TPU v7x, 256 devices: a whole 4x4x8 slice. The times are simulated.
256 devices in a mesh: dp: 32 (over z, x), mp: 8 (over y, core).
Axes of the slice: x: 4, y: 4, z: 8, core: 2. Of those that a mesh axis runs over, the one named last changes fastest.
Arguments:
- attn: bfloat16 [2, 4096, 4096], P(None, 'dp', 'mp'), may hold values from -6 to 6
- stream: bfloat16 [2, 4096, 4096], P(None, 'dp', 'mp'), may hold values from -13 to 13
- out_proj: bfloat16 [4096, 4096], P(None, 'mp'), may hold values from -0.09375 to 0.09375
- gain: float32 [4096], P('mp'), may hold values from 0.25 to 1.75
- neg_owner: int32 [4096, 8], P('dp'), may hold values from 0 to 31, as said below
- neg_row: int32 [4096, 8], P('dp'), may hold values from 0 to 127
Outputs:
- query_loss: float32 [4096], P('dp')
- grad_stream: float32 [2, 4096, 4096], P(None, 'dp', 'mp')
- grad_attn: float32 [2, 4096, 4096], P(None, 'dp', 'mp')
- grad_out_proj: float32 [4096, 4096], P('dp', 'mp')
Inputs may be any that keep to these rules, and one draw needn't show every extreme that they name: `neg_owner`: the 8 hard negatives of a query have distinct owners; among the 128 queries of one index of dp, no owner is named more than 64 times.
All inputs are finite; a program needn't handle non-finite values.
Results may differ from a plain program's by a relative error of at most 0.018.
Values may be sent and summed in bfloat16 or wider, within the bound.
No kernel may reach another device: no remote copies, remote signals or barrier semaphores. Data moves between devices by JAX's collectives and lax.ppermute only.
A program may use at most 64 MiB of HBM per device.

v0:
```python
import jax
import jax.numpy as jnp
from jax import lax
from jax.experimental import pallas as pl
from jax.experimental.pallas import tpu as pltpu
from jax.sharding import Mesh
from jax.sharding import PartitionSpec as P

WARMTH = 0.02
GRAD_SCALE = 16.0 / WARMTH
EPSILON = 1e-06
F32 = jnp.float32
BF16 = jnp.bfloat16
DP = ("z", "x")
MP = ("y", "core")
NZ, NX, NY, NC = 8, 4, 4, 2
N_DP, N_MP = NZ * NX, NY * NC
ROWS = 128
NEG = 8
ALL_ROWS = N_DP * ROWS
FEATURES = 512
WIDTH = N_MP * FEATURES
TILE = 1024
CHUNK = 4


def shifted(size, step):
    return [(i, (i + step) % size) for i in range(size)]


def place(buffer, block, index):
    return lax.dynamic_update_slice(buffer, block[None], (index,) + (0,) * block.ndim)


def gather_x(block):
    x = lax.axis_index("x")
    parts = [lax.ppermute(block, "x", shifted(NX, s)) for s in (1, 3, 2)]
    buffer = jnp.zeros((NX,) + block.shape, block.dtype)
    for s, part in zip((0, 1, 3, 2), [block] + parts):
        buffer = place(buffer, part, (x - s) % NX)
    return buffer


def pieces_x(line):
    left = lax.ppermute(line, "x", shifted(NX, 1))
    right = lax.ppermute(line, "x", shifted(NX, -1))
    low = lax.ppermute(left[: NZ // 2], "x", shifted(NX, 1))
    high = lax.ppermute(right[NZ // 2 :], "x", shifted(NX, -1))
    return line, left, right, low, high


PLACES_X = (0, 1, 3, 2)
DEEP = 2
LATE = 32


def late_rows(ref, j):
    r = ref[pl.ds(j, 1)].astype(F32)[0]
    return r[:8], r[8:16] + r[16:24], r[24:25] + r[25:26], r[26:27], r[27:28] + r[28:29], r[29:30] + r[30:31]


def index_rows(ref, j):
    r = ref[:, pl.ds(j, 1)].astype(F32)[:, 0]
    return r[:, 0].astype(jnp.int32), r[:, 1].astype(jnp.int32)


def shares_spec(groups, part, size=16):
    return pl.BlockSpec((N_MP, groups, size, ROWS), lambda t: (0, t, part, 0))


def piece_specs():
    block = (DEEP, ROWS, FEATURES)
    half = NZ // 2 // DEEP
    near = pl.BlockSpec(block, lambda t: (t, 0, 0))
    low = pl.BlockSpec(block, lambda t: (jnp.minimum(t, half - 1), 0, 0))
    high = pl.BlockSpec(block, lambda t: (jnp.maximum(t - half, 0), 0, 0))
    return [near, near, near, low, high]


def read_pieces(refs):
    line, left, right, low, high = refs
    is_low = pl.program_id(0) < NZ // 2 // DEEP
    rows = []
    for i in range(DEEP):
        rows += [line[i], left[i], right[i], jnp.where(is_low, low[i], high[i])]
    return jnp.concatenate(rows, axis=0)


def spread_dp(block):
    copies = jnp.broadcast_to(block[None], (N_DP,) + block.shape)
    return lax.all_to_all(copies, DP, 0, 0, tiled=True)


HALF = N_DP // 2


def coef_kernel(
    core_ref, index_ref, late_ref, exps_ref, aq_ref, ap_ref, invp_ref, whole_ref, left_ref, xp_ref,
    xq, apt_ref,
):
    step = pl.program_id(0)
    groups = TILE // ROWS
    core = core_ref[0]
    held = lambda o: ap_ref[:, pl.ds(core * HALF + o, 1)].reshape(ROWS, ROWS)

    @pl.when(step == 0)
    def _():
        xq[...] = jnp.zeros_like(xq)
        for o in range(HALF):
            apt_ref[:, o * ROWS : (o + 1) * ROWS] = held(o).astype(F32).T.astype(BF16)

    lates = [late_rows(late_ref, g) for g in range(groups)]
    indices = [index_rows(index_ref, g) for g in range(groups)]
    beside = lambda rows, i: jnp.concatenate([r[i] for r in rows], axis=1)
    hard_k, carried_k = beside(lates, 0), beside(lates, 1)
    owner, row = beside(indices, 0) - core * HALF, beside(indices, 1)
    aq = jnp.concatenate([aq_ref[:, g].reshape(ROWS, ROWS) for g in range(groups)], axis=0)
    order = lax.broadcasted_iota(jnp.int32, (HALF, TILE), 0)
    named = jnp.full((HALF, TILE), -1, jnp.int32)
    hard = jnp.zeros((HALF, TILE), F32)
    carried = jnp.zeros((HALF, TILE), F32)
    for k in range(NEG):
        hit = owner[k : k + 1] == order
        named = jnp.where(hit, row[k : k + 1], named)
        hard = jnp.where(hit, hard_k[k : k + 1], hard)
        carried = jnp.where(hit, carried_k[k : k + 1], carried)
    high = carried.astype(BF16)
    low = (carried - high.astype(F32)).astype(BF16)
    pad = jnp.zeros((ROWS - 2 * HALF, TILE), F32)
    extra = jnp.concatenate([high.astype(F32), low.astype(F32), pad], axis=0).T.astype(BF16)
    aq_ext = jnp.concatenate([aq, extra], axis=1)
    row_of = lax.broadcasted_iota(jnp.int32, (ROWS, TILE), 0)
    xp = jnp.zeros((ROWS, TILE), F32)
    for c in range(0, HALF, CHUNK):
        tiles = []
        for o in range(c, c + CHUNK):
            tile = jnp.where(row_of == named[o : o + 1], hard[o : o + 1], 0.0)
            tiles.append(tile.astype(BF16))
        coef = jnp.concatenate(tiles, axis=0)
        at = slice(c * ROWS, (c + CHUNK) * ROWS)
        xq[at, :] += jnp.dot(coef, aq_ext, preferred_element_type=F32)
        xp = xp + jnp.dot(apt_ref[:, at], coef, preferred_element_type=F32)
    xp_ref[...] = xp.astype(BF16)

    eye = lax.broadcasted_iota(jnp.int32, (ROWS, ROWS), 0) == lax.broadcasted_iota(
        jnp.int32, (ROWS, ROWS), 1
    )

    @pl.when(step // (HALF // groups) == core)
    def _():
        for part in range(groups):
            lanes = slice(part * ROWS, (part + 1) * ROWS)
            exps = exps_ref[:, part].reshape(ROWS, ROWS).astype(F32)
            inner = jnp.where(eye, lates[part][3], exps * lates[part][2]).astype(BF16)
            at = pl.ds(pl.multiple_of((step * groups + part - core * HALF) * ROWS, ROWS), ROWS)
            xq[at, :ROWS] += jnp.dot(inner, aq[lanes, :], preferred_element_type=F32)
            more = jnp.dot(apt_ref[:, at], inner, preferred_element_type=F32)
            more = more - aq[lanes, :].astype(F32).T * lates[part][4]
            xp_ref[:, lanes] = (xp_ref[:, lanes].astype(F32) + more).astype(BF16)

    @pl.when(step == pl.num_programs(0) - 1)
    def _():
        lane = lax.broadcasted_iota(jnp.int32, (ROWS, ROWS), 1)
        for o in range(HALF):
            at = slice(o * ROWS, (o + 1) * ROWS)
            sums = xq[at, ROWS:]
            mine = (lane == o) | (lane == HALF + o)
            hard_sum = jnp.sum(jnp.where(mine, sums, 0.0), axis=1, keepdims=True)
            across = lambda v: jnp.sum(jnp.where(eye, v, 0.0), axis=1, keepdims=True)
            all_o = core * HALF + o
            cp = hard_sum * across(invp_ref[pl.ds(all_o, 1), :]) + across(late_rows(whole_ref, all_o)[5])
            left_ref[at, :] = (xq[at, :ROWS] - held(o).astype(F32) * cp).astype(BF16)

def coefficients(core, shares, late, invp):
    full = lambda shape: pl.BlockSpec(shape, lambda t: (0,) * len(shape))
    held = HALF * ROWS
    groups = TILE // ROWS
    return pl.pallas_call(
        coef_kernel,
        grid=(ALL_ROWS // TILE,),
        in_specs=[
            pl.BlockSpec(memory_space=pltpu.SMEM), shares_spec(groups, 6, 8),
            pl.BlockSpec((groups, LATE, ROWS), lambda t: (t, 0, 0)),
            shares_spec(groups, 2), shares_spec(groups, 0),
            pl.BlockSpec((N_MP, N_DP, 16, ROWS), lambda t: (0, 0, 1, 0)), full((N_DP, ROWS)),
            full((N_DP, LATE, ROWS)),
        ],
        out_specs=[full((held, ROWS)), pl.BlockSpec((ROWS, TILE), lambda t: (0, t))],
        out_shape=[
            jax.ShapeDtypeStruct((held, ROWS), BF16),
            jax.ShapeDtypeStruct((ROWS, ALL_ROWS), BF16),
        ],
        scratch_shapes=[
            pltpu.VMEM((held, 2 * ROWS), F32),
            pltpu.VMEM((ROWS, held), BF16),
        ],
        compiler_params=pltpu.CompilerParams(vmem_limit_bytes=56 * 2**20),
        cost_estimate=pl.CostEstimate(
            flops=10 * 10**9, bytes_accessed=8 * 2**20, transcendentals=0
        ),
        name="coefficients",
    )(core.reshape(1), shares, late, shares, shares, shares, invp, late)

def own_kernel(
    d_ref, owner_ref, row_ref, hard_ref, inner_ref, index_ref, late_ref, sq_ref, sp_ref,
    gain_ref, cq_ref, tin_ref, invp_ref, q_ref, p0, p1, p2, p3, p4, stream_ref, rounded_ref,
    acc_q, acc_p, acc_t,
):
    step = pl.program_id(0)
    d, x = d_ref[0], d_ref[1]

    @pl.when(step == 0)
    def _():
        acc_q[...] = jnp.zeros_like(acc_q)
        acc_p[...] = jnp.zeros_like(acc_p)
        acc_t[...] = jnp.zeros_like(acc_t)

    row_of = lax.broadcasted_iota(jnp.int32, (ROWS, ROWS), 0)
    down = lambda v: jnp.sum(v, axis=0, keepdims=True)
    tall, wide = [], []
    for g in range(DEEP * NX):
        plane, n = step * DEEP + g // NX, g % NX
        block = plane * NX + (x + NX - PLACES_X[n]) % NX
        inner = jnp.where(block == d, inner_ref[...], 0.0)
        hit = owner_ref[...] == block
        named = down(jnp.where(hit, row_ref[...] + 1, 0)) - 1
        hard = down(jnp.where(hit, hard_ref[...], 0.0))
        tall.append((jnp.where(row_of == named, hard, 0.0) + inner).astype(BF16))
        inner = jnp.where(plane * NX + n == d, inner_ref[...], 0.0)
        owners, rows = index_rows(index_ref, g)
        hard_k, carried_k = late_rows(late_ref, g)[:2]
        hit = owners == d
        named = row_of == down(jnp.where(hit, rows + 1, 0)) - 1
        hard = down(jnp.where(hit, hard_k, 0.0))
        moved = down(jnp.where(hit, hard_k * carried_k, 0.0))
        wide.append((jnp.where(named, hard, 0.0) + inner).astype(BF16))
        acc_t[...] += jnp.where(named, moved, 0.0)
    acc_q[...] += lax.dot_general(
        jnp.concatenate(tall, axis=0), read_pieces((p0, p1, p2, p3, p4)), (((0,), (0,)), ((), ())),
        preferred_element_type=F32,
    )
    acc_p[...] += jnp.dot(jnp.concatenate(wide, axis=1), q_ref[...], preferred_element_type=F32)

    @pl.when(step == pl.num_programs(0) - 1)
    def _():
        eye = row_of == lax.broadcasted_iota(jnp.int32, (ROWS, ROWS), 1)
        across = lambda ref: jnp.sum(jnp.where(eye, ref[...], 0.0), axis=1, keepdims=True)
        cp = across(tin_ref) + jnp.sum(acc_t[...], axis=1, keepdims=True) * across(invp_ref)
        grad_q = gain_ref[...] * (acc_q[...] - across(cq_ref) * sq_ref[...])
        grad_p = gain_ref[...] * (acc_p[...] - cp * sp_ref[...])
        stream_ref[:ROWS, :] = grad_q
        stream_ref[ROWS:, :] = grad_p
        rounded_ref[:ROWS, :] = grad_q.astype(BF16)
        rounded_ref[ROWS:, :] = grad_p.astype(BF16)


def own_gradients(at, owner, row, hard, inner, shares, late, sq, sp, gain, cq, tin, invp, q, p):
    full = lambda a: pl.BlockSpec(a.shape, lambda t: (0,) * a.ndim)
    size = DEEP * NX
    tall = pl.BlockSpec((size * ROWS, FEATURES), lambda t: (t, 0))
    whole = pl.BlockSpec((2 * ROWS, FEATURES), lambda t: (0, 0))
    return pl.pallas_call(
        own_kernel,
        grid=(NZ // DEEP,),
        in_specs=[pl.BlockSpec(memory_space=pltpu.SMEM)]
        + [full(a) for a in (owner, row, hard, inner)]
        + [shares_spec(size, 6, 8), pl.BlockSpec((size, LATE, ROWS), lambda t: (t, 0, 0))]
        + [full(a) for a in (sq, sp, gain, cq, tin, invp)]
        + [tall]
        + piece_specs(),
        out_specs=[whole, whole],
        out_shape=[
            jax.ShapeDtypeStruct((2 * ROWS, FEATURES), F32),
            jax.ShapeDtypeStruct((2 * ROWS, FEATURES), BF16),
        ],
        scratch_shapes=[
            pltpu.VMEM((ROWS, FEATURES), F32),
            pltpu.VMEM((ROWS, FEATURES), F32),
            pltpu.VMEM((ROWS, ROWS), F32),
        ],
        compiler_params=pltpu.CompilerParams(vmem_limit_bytes=56 * 2**20),
        cost_estimate=pl.CostEstimate(
            flops=2 * 10**9, bytes_accessed=10 * 2**20, transcendentals=0
        ),
        name="own_gradients",
    )(at, owner, row, hard, inner, shares, late, sq, sp, gain, cq, tin, invp, q, *p)


def final_kernel(
    x_ref, left_ref, near_ref, far_ref, gain_ref, q_ref, p0, p1, p2, p3, p4, out_ref
):
    step = pl.program_id(0)
    x = x_ref[0]

    @pl.when(step == 0)
    def _():
        out_ref[...] = jnp.zeros_like(out_ref)

    starts = [
        pl.multiple_of((i * NX + (x + NX - s) % NX) * ROWS, ROWS) for i in range(DEEP) for s in PLACES_X
    ]
    left = jnp.concatenate([left_ref[pl.ds(start, ROWS), :] for start in starts], axis=0)
    right = (near_ref[...].astype(F32) + far_ref[...].astype(F32)).astype(BF16)
    out_ref[...] += gain_ref[...] * (
        lax.dot_general(
            left, read_pieces((p0, p1, p2, p3, p4)), (((0,), (0,)), ((), ())),
            preferred_element_type=F32,
        )
        + jnp.dot(right, q_ref[...], preferred_element_type=F32)
    )


def final_product(at, left, near, far, gain, q, p):
    size = DEEP * NX * ROWS
    lanes = lambda n: pl.BlockSpec((n, size), lambda t: (0, t))
    tall = lambda n: pl.BlockSpec((size, n), lambda t: (t, 0))
    return pl.pallas_call(
        final_kernel,
        grid=(NZ // DEEP,),
        in_specs=[
            pl.BlockSpec(memory_space=pltpu.SMEM), tall(ROWS), lanes(ROWS), lanes(ROWS),
            pl.BlockSpec((1, FEATURES), lambda t: (0, 0)), tall(FEATURES),
        ]
        + piece_specs(),
        out_specs=pl.BlockSpec((ROWS, FEATURES), lambda t: (0, 0)),
        out_shape=jax.ShapeDtypeStruct((ROWS, FEATURES), F32),
        compiler_params=pltpu.CompilerParams(vmem_limit_bytes=56 * 2**20),
        cost_estimate=pl.CostEstimate(
            flops=2 * 10**9, bytes_accessed=12 * 2**20, transcendentals=0
        ),
        name="final_product",
    )(at, left, near, far, gain, q, *p)


STEPS_Y = (0, 1, 3, 2)


def body(attn, stream, out_proj, gain, neg_owner, neg_row):
    z, x = lax.axis_index("z"), lax.axis_index("x")
    y, core = lax.axis_index("y"), lax.axis_index("core")
    d, m = z * NX + x, y * NC + core

    blocks = out_proj.reshape(NY, NC, FEATURES, FEATURES)

    def by_core(c):
        kept = [
            lax.dynamic_slice(blocks, ((y - s) % NY, c, 0, 0), (1, 1, FEATURES, FEATURES))
            for s in STEPS_Y
        ]
        return jnp.concatenate(kept, axis=0).reshape(NY * FEATURES, FEATURES)

    proj_mine, proj_other = by_core(core), by_core(1 - core)

    def project(block, kind):
        parts = [block] + [lax.ppermute(block, "y", shifted(NY, s)) for s in STEPS_Y[1:]]
        near = jnp.concatenate(parts, axis=1)
        far = lax.ppermute(near, "core", shifted(NC, 1))
        hidden = jnp.dot(near, proj_mine, preferred_element_type=F32)
        hidden = hidden + jnp.dot(far, proj_other, preferred_element_type=F32)
        scaled = (hidden + stream[kind].astype(F32)) * gain[None, :]
        return (near, far), scaled, scaled.astype(BF16)

    pair_p, scaled_p, passages = project(attn[1], 1)
    p_line = lax.all_gather(passages, "z", axis=0)
    p_pieces = pieces_x(p_line)

    attn_q, _ = lax.optimization_barrier((attn[0], passages))
    pair_q, scaled_q, queries = project(attn_q, 0)
    column = gather_x(queries).reshape(NX * ROWS, FEATURES)
    q_all = lax.all_gather(column, "z", axis=0, tiled=True)

    def some_rows(pair):
        cut = [lax.dynamic_slice_in_dim(v, m * 16, 16, 0).reshape(16, NY, FEATURES) for v in pair]
        both = jnp.stack([jnp.where(core == 0, cut[c], cut[1 - c]) for c in range(NC)])
        at = lambda a: jnp.where((y - a) % NY == 3, 2, jnp.where((y - a) % NY == 2, 3, (y - a) % NY))
        rows = [lax.dynamic_index_in_dim(both, at(a), 2, keepdims=False) for a in range(NY)]
        return jnp.stack(rows)

    mine = jnp.stack([some_rows(pair_q), some_rows(pair_p)])
    mine = mine.reshape(2, NZ, 16, NX, ROWS).transpose(1, 3, 0, 2, 4).reshape(N_DP, 32, ROWS)

    owner, row = neg_owner.T, neg_row.T
    order = jnp.arange(N_DP, dtype=jnp.int32)

    def dense(owners, values, empty):
        hit = owners[None] == order.reshape((N_DP,) + (1,) * owners.ndim)
        return jnp.sum(jnp.where(hit, values[None] - empty, 0), axis=1) + empty

    rows_own = dense(owner, row, -1)

    inner_part = lax.dot_general(
        passages, queries, (((1,), (1,)), ((), ())), preferred_element_type=F32
    )
    squares = jnp.stack([jnp.sum(scaled_q * scaled_q, axis=1), jnp.sum(scaled_p * scaled_p, axis=1)])
    part = jnp.concatenate([inner_part, squares, jnp.zeros((6, ROWS), F32)], axis=0)
    part, _ = lax.optimization_barrier((part, column))
    total = jnp.sum(lax.all_gather(part, MP, axis=0), axis=0)
    norm_q = jnp.sqrt(total[ROWS] + EPSILON)
    norm_p = jnp.sqrt(total[ROWS + 1] + EPSILON)
    inv_q, inv_p = 1.0 / norm_q, 1.0 / norm_p
    score = total[:ROWS] * inv_p[:, None] * inv_q[None, :]
    logit = score / WARMTH
    eye = jnp.eye(ROWS, dtype=bool)
    positive = jnp.sum(jnp.where(eye, logit, 0.0), axis=0)
    top = jnp.max(logit, axis=0)
    exps = jnp.exp(logit - top[None, :])
    exp_sum = jnp.sum(exps, axis=0)
    exps = (exps * inv_p[:, None] * inv_q[None, :]).astype(BF16)

    ids = (owner * ROWS + row)[m % NEG]
    high = lax.reduce_precision(inv_p, 8, 7)
    middle = lax.reduce_precision(inv_p - high, 8, 7)
    small = [(ids // ROWS), (ids % ROWS), high, middle, inv_p - high - middle]
    share = jnp.concatenate(
        [
            lax.dynamic_slice_in_dim(exps, m * 16, 16, 0),
            jnp.stack([v.astype(BF16) for v in small]),
            jnp.zeros((3, ROWS), BF16),
        ],
        axis=0,
    )
    share = jnp.concatenate([mine, jnp.broadcast_to(share[None], (N_DP, 24, ROWS))], axis=1)
    share, _ = lax.optimization_barrier((share, p_line))
    share = lax.all_to_all(share, DP, 0, 0, tiled=True)
    invp_all = jnp.sum(share[:, 50:53].astype(F32), axis=1)
    shares = lax.all_gather(share, MP, axis=0)

    row_iota = jnp.arange(ROWS, dtype=jnp.int32)
    named = rows_own[:, None, :] == row_iota[None, :, None]
    invp_named = jnp.sum(jnp.where(named, invp_all[:, :, None], 0.0), axis=1)
    raw_hard = jnp.zeros((NEG, ROWS), F32)
    for piece, s, first in zip(p_pieces, (0, 1, 3, 2, 2), (0, 0, 0, 0, NZ // 2)):
        here = (first + jnp.arange(piece.shape[0])) * NX + (x - s) % NX
        hit = owner[None] == here[:, None, None]
        row_here = jnp.sum(jnp.where(hit, row[None] + 1, 0), axis=1) - 1
        raw = lax.dot_general(
            piece.reshape(-1, FEATURES), queries, (((1,), (1,)), ((), ())), preferred_element_type=F32
        ).reshape(-1, ROWS, ROWS)
        raw = jnp.sum(jnp.where(row_here[:, None] == row_iota[None, :, None], raw, 0.0), axis=1)
        raw_hard = raw_hard + jnp.sum(jnp.where(hit, raw[:, None], 0.0), axis=0)

    def pick(values):
        hit = owner[:, None, :] == order[None, :, None]
        return jnp.sum(jnp.where(hit, values[None], 0.0), axis=1)

    invp_hard = pick(invp_named)
    copies = jnp.broadcast_to(raw_hard[None], (N_MP, NEG, ROWS))
    raw = jnp.sum(lax.all_to_all(copies, MP, 0, 0, tiled=True), axis=0)
    hard_score = raw * invp_hard * inv_q[None]
    hard_logit = hard_score / WARMTH
    peak = jnp.maximum(top, jnp.max(hard_logit, axis=0))
    log_total = peak + jnp.log(
        exp_sum * jnp.exp(top - peak) + jnp.sum(jnp.exp(hard_logit - peak[None]), axis=0)
    )
    query_loss = log_total - positive
    hard = GRAD_SCALE * jnp.exp(hard_logit - log_total[None]) * inv_q[None] * invp_hard
    hard = hard.astype(BF16).astype(F32)
    factor = GRAD_SCALE * jnp.exp(top - log_total)
    diag = GRAD_SCALE * (jnp.exp(positive - log_total) - 1.0) * inv_q * inv_p
    inner = jnp.where(eye, diag[None], exps.astype(F32) * factor[None])
    inner_rounded = inner.astype(BF16).astype(F32)
    weighted = inner_rounded * score * norm_p[:, None]
    is_own = owner == d
    cq = (jnp.sum(weighted, axis=0) + jnp.sum(hard * hard_score / invp_hard, axis=0)) * inv_q
    own_row = jnp.sum(jnp.where(is_own, row + 1, 0), axis=0) - 1
    own_hard = jnp.sum(jnp.where(is_own, hard * hard_score, 0.0), axis=0)
    inner_p = inner_rounded * score + jnp.where(row_iota[:, None] == own_row[None], own_hard[None], 0.0)
    tin = jnp.sum(inner_p * norm_q[None], axis=1) * inv_p
    carried = jnp.where(is_own, 0.0, hard_score * norm_q[None])

    def pieces(v):
        high = lax.reduce_precision(v, 8, 7)
        return [high, v - high]

    late = [hard] + pieces(carried) + [jnp.stack(pieces(factor) + [diag] + pieces(cq) + pieces(tin) + [diag])]
    late = jnp.concatenate([v.astype(BF16) for v in late], axis=0)
    late_half = lax.dynamic_slice_in_dim(late, core * (LATE // 2), LATE // 2, 0)
    late_half = spread_dp(late_half)
    late_other = lax.ppermute(late_half, "core", shifted(NC, 1))
    late_all = jnp.concatenate(
        [jnp.where(core == 0, late_half, late_other), jnp.where(core == 0, late_other, late_half)],
        axis=1,
    )

    line = lambda v: v.reshape(1, -1)
    grad_stream, rounded = own_gradients(
        jnp.stack([d, x]), owner, row, hard, inner, shares, late_all, scaled_q, scaled_p,
        line(gain), line(cq), line(tin), line(inv_p), q_all, p_pieces,
    )

    back = lambda w: lax.dot_general(
        rounded, w, (((1,), (1,)), ((), ())), preferred_element_type=F32
    )
    came = lax.ppermute(back(proj_other).astype(BF16), "core", shifted(NC, 1))
    kept = back(proj_mine) + came.astype(F32)
    grad_attn = kept[:, :FEATURES]
    for i, s in list(enumerate(STEPS_Y))[1:]:
        block = kept[:, i * FEATURES : (i + 1) * FEATURES].astype(BF16)
        grad_attn = grad_attn + lax.ppermute(block, "y", shifted(NY, -s)).astype(F32)

    late_used, _ = lax.optimization_barrier((late_all, kept))
    left, right = coefficients(core, shares, late_used, invp_all)
    left_other = lax.ppermute(left, "core", shifted(NC, 1))
    right_other = lax.ppermute(right, "core", shifted(NC, 1))
    left = jnp.concatenate(
        [jnp.where(core == 0, left, left_other), jnp.where(core == 0, left_other, left)], axis=0
    )
    grad_weight = final_product(
        x.reshape(1), left, right, right_other, line(gain), q_all, p_pieces
    )
    return (
        query_loss,
        grad_stream.reshape(2, ROWS, FEATURES),
        grad_attn.reshape(2, ROWS, FEATURES),
        grad_weight,
    )


def solution(mesh):
    fine = Mesh(mesh.devices.reshape(NZ, NX, NY, NC), ("z", "x", "y", "core"))
    placed = (
        P(None, DP, MP),
        P(None, DP, MP),
        P(None, MP),
        P(MP),
        P(DP, None),
        P(DP, None),
    )
    return jax.shard_map(
        body,
        mesh=fine,
        in_specs=placed,
        out_specs=(P(DP), P(None, DP, MP), P(None, DP, MP), P(DP, MP)),
        check_vma=False,
    )
```

profile of v0, /device:TPU:1, one launch (start us, length us, event | category | flops | bytes accessed | tf_op | source)
XLA Modules:
  0.0 217.4 jit_solution(8131139685151138075)
XLA Ops:
  7.2 1.0 slice_bitcast_fusion
  8.2 3.8 %collective-permute-start.2 = (bf16[128,512]{1,0:T(8,128)(2,1)S(1)}, bf16[128,512]{1,0:T(8,128)(2,1)S(1)}, u32[]{:S(2)}, u32[]{:S(2)}) collective-permute-start(bf16[128,512]{1,0:T(8,128)(2,1)S(1)} %get-tuple-element.78), channel_id=1, source_target_pairs={{0,4},{2,6},{4,0},{6,2},{1,5},{3,7},{5,1},{7,3},{8,12},{10,14},{12... | collective-permute-start | bytes 393224 | tf_op jit(solution)/shard_map/ppermute | solution.py:355
  13.5 0.9 collective-permute-done.2
  14.4 3.7 %collective-permute-done.1 = bf16[128,512]{1,0:T(8,128)(2,1)S(1)} collective-permute-done((bf16[128,512]{1,0:T(8,128)(2,1)S(1)}, bf16[128,512]{1,0:T(8,128)(2,1)S(1)}, u32[]{:S(2)}, u32[]{:S(2)}) %collective-permute-start.1) | collective-permute-done | bytes 131104 | tf_op jit(solution)/shard_map/ppermute | solution.py:355
  18.1 1.9 collective-permute-done
  20.1 1.1 collective-permute-start.3
  21.2 2.4 %constant_dynamic-slice_fusion.18 = (bf16[1,1,512,512]{3,2,1,0:T(8,128)(2,1)S(1)}, bf16[1,1,512,512]{3,2,1,0:T(8,128)(2,1)S(1)}, bf16[1,1,512,512]{3,2,1,0:T(8,1...) fusion(bf16[4,2,512,512]{3,2,1,0:T(8,128)(2,1)} %bitcast.169, ...), kind=kLoop, calls=%fused_computation.132 | loop fusion | bytes 8388632 | tf_op jit(solution)/shard_map/dynamic_slice | solution.py:347
  25.4 1.8 fusion.54
  27.2 2.2 %collective-permute-start.6 = (bf16[128,512]{1,0:T(8,128)(2,1)S(1)}, bf16[128,512]{1,0:T(8,128)(2,1)S(1)}, u32[]{:S(2)}, u32[]{:S(2)}) collective-permute-start(bf16[128,512]{1,0:T(8,128)(2,1)S(1)} %get-tuple-element.12), channel_id=1, source_target_pairs={{0,4},{2,6},{4,0},{6,2},{1,5},{3,7},{5,1},{7,3},{8,12},{10,14},{12... | collective-permute-start | bytes 393224 | tf_op jit(solution)/shard_map/ppermute | solution.py:355
  29.4 1.1 collective-permute-start.5
  30.5 3.4 %collective-permute-done.4 = bf16[128,512]{1,0:T(8,128)(2,1)S(1)} collective-permute-done((bf16[128,512]{1,0:T(8,128)(2,1)S(1)}, bf16[128,512]{1,0:T(8,128)(2,1)S(1)}, u32[]{:S(2)}, u32[]{:S(2)}) %collective-permute-start.4) | collective-permute-done | bytes 131104 | tf_op jit(solution)/shard_map/ppermute | solution.py:355
  33.9 2.6 %collective-permute-done.5 = bf16[128,512]{1,0:T(8,128)(2,1)S(1)} collective-permute-done((bf16[128,512]{1,0:T(8,128)(2,1)S(1)}, bf16[128,512]{1,0:T(8,128)(2,1)S(1)}, u32[]{:S(2)}, u32[]{:S(2)}) %collective-permute-start.5) | collective-permute-done | bytes 131104 | tf_op jit(solution)/shard_map/ppermute | solution.py:355
  36.6 1.3 collective-permute-start.7
  37.9 1.4 collective-permute-done.7
  41.8 2.4 %collective-permute-start.10 = (bf16[128,512]{1,0:T(8,128)(2,1)S(1)}, bf16[128,512]{1,0:T(8,128)(2,1)S(1)}, u32[]{:S(2)}, u32[]{:S(2)}) collective-permute-start(bf16[128,512]{1,0:T(8,128)(2,1)S(1)} %get-tuple-element.55), channel_id=1, source_target_pairs={{0,16},{8,24},{16,0},{24,8},{1,17},{9,25},{17,1},{25,9},{2,18},{10... | collective-permute-start | bytes 393224 | tf_op jit(solution)/shard_map/ppermute | solution.py:37
  44.2 1.2 collective-permute-start.9
  45.3 2.1 collective-permute-done.8
  47.4 0.9 bitcast_dynamic-update-slice_fusion.2
  48.3 2.0 collective-permute-done.9
  53.1 0.9 broadcast_select_fusion.4
  54.6 0.9 broadcast_select_fusion.6
  56.6 14.7 %all-gather = f32[1088,128]{1,0:T(8,128)S(1)} all-gather(f32[136,128]{1,0:T(8,128)S(1)} %maximum_maximum_fusion), channel_id=2, replica_groups=mesh['z'=8,'x'=4,'y'=4,'core'=2] {'y','core'}, dimensions={0}, use_global_device_ids=true | all-gather | bytes 626688 | tf_op jit(solution)/shard_map/all_gather | solution.py:397
  73.4 10.0 %all-to-all-start.1 = ((bf16[32,56,128]{2,1,0:T(8,128)(2,1)}), bf16[32,56,128]{2,1,0:T(8,128)(2,1)S(1)}, u32[]{:S(2)}, u32[]{:S(2)}) async-start(bf16[32,56,128]{2,1,0:T(8,128)(2,1)} %pad_maximum_fusion.4), calls=%async_computation.1 | async-start | bytes 917504 | tf_op jit(solution)/shard_map/all_to_all | solution.py:424
  83.6 13.5 %all-to-all-done.1 = bf16[32,56,128]{2,1,0:T(8,128)(2,1)S(1)} async-done(((bf16[32,56,128]{2,1,0:T(8,128)(2,1)}), bf16[32,56,128]{2,1,0:T(8,128)(2,1)S(1)}, u32[]{:S(2)}, u32[]{:S(2)}) %all-to-all-start.1) | async-done | bytes 458784 | tf_op jit(solution)/shard_map/all_to_all | solution.py:424
  98.1 2.7 %collective-permute-start.12 = (bf16[8,128,512]{2,1,0:T(8,128)(2,1)}, bf16[8,128,512]{2,1,0:T(8,128)(2,1)S(1)}, u32[]{:S(2)}, u32[]{:S(2)}) collective-permute-start(bf16[8,128,512]{2,1,0:T(8,128)(2,1)} %bitcast.164), channel_id=1, source_target_pairs={{0,24},{8,0},{16,8},{24,16},{1,25},{9,1},{17,9},{25,17},{2,26},{10... | collective-permute-start | bytes 3145736 | tf_op jit(solution)/shard_map/ppermute | solution.py:46
  100.8 1.7 fusion
  102.5 0.9 convert_reduce_fusion.invp_ref
  103.4 14.1 %collective-permute-done.12.p2 = bf16[8,128,512]{2,1,0:T(8,128)(2,1)S(1)} collective-permute-done((bf16[8,128,512]{2,1,0:T(8,128)(2,1)}, bf16[8,128,512]{2,1,0:T(8,128)(2,1)S(1)}, u32[]{:S(2)}, u32[]{:S(2)}) %collective-permute-start.12) | collective-permute-done | bytes 1048608 | tf_op jit(solution)/shard_map/ppermute | solution.py:46
  117.6 3.5 %collective-permute-start.14 = (bf16[4,128,512]{2,1,0:T(8,128)(2,1)S(1)}, bf16[4,128,512]{2,1,0:T(8,128)(2,1)S(1)}, u32[]{:S(2)}, u32[]{:S(2)}) collective-permute-start(bf16[4,128,512]{2,1,0:T(8,128)(2,1)S(1)} %slice.63), channel_id=1, source_target_pairs={{0,24},{8,0},{16,8},{24,16},{1,25},{9,1},{17,9},{25,17},{2,26},{10... | collective-permute-start | bytes 1572872 | tf_op jit(solution)/shard_map/ppermute | solution.py:48
  121.8 1.1 slice.62
  123.4 1.7 fusion.1
  125.2 4.3 %collective-permute-done.14.p4 = bf16[4,128,512]{2,1,0:T(8,128)(2,1)S(1)} collective-permute-done((bf16[4,128,512]{2,1,0:T(8,128)(2,1)S(1)}, bf16[4,128,512]{2,1,0:T(8,128)(2,1)S(1)}, u32[]{:S(2)}, u32[]{:S(2)}) %collective-permute-start.14) | collective-permute-done | bytes 524320 | tf_op jit(solution)/shard_map/ppermute | solution.py:48
  130.6 2.4 %collective-permute-done.13.p3 = bf16[4,128,512]{2,1,0:T(8,128)(2,1)S(1)} collective-permute-done((bf16[4,128,512]{2,1,0:T(8,128)(2,1)S(1)}, bf16[4,128,512]{2,1,0:T(8,128)(2,1)S(1)}, u32[]{:S(2)}, u32[]{:S(2)}) %collective-permute-start.13) | collective-permute-done | bytes 524320 | tf_op jit(solution)/shard_map/ppermute | solution.py:47
  134.9 13.7 %all-to-all-start = ((f32[8,8,128]{2,1,0:T(8,128)}), f32[8,8,128]{2,1,0:T(8,128)S(1)}, u32[]{:S(2)}, u32[]{:S(2)}) async-start(f32[8,8,128]{2,1,0:T(8,128)} %broadcast_in_dim.276), calls=%async_computation | async-start | bytes 65536 | tf_op jit(solution)/shard_map/all_to_all | solution.py:448
  148.6 4.7 %all-to-all-done = f32[8,8,128]{2,1,0:T(8,128)S(1)} async-done(((f32[8,8,128]{2,1,0:T(8,128)}), f32[8,8,128]{2,1,0:T(8,128)S(1)}, u32[]{:S(2)}, u32[]{:S(2)}) %all-to-all-start) | async-done | bytes 32800 | tf_op jit(solution)/shard_map/all_to_all | solution.py:448
  154.4 12.4 %all_to_all.15 = bf16[32,16,128]{2,1,0:T(8,128)(2,1)S(1)} all-to-all(bf16[32,16,128]{2,1,0:T(8,128)(2,1)S(1)} %broadcast_in_dim.291), channel_id=1, replica_groups=mesh['z'=8,'x'=4,'y'=4,'core'=2] {'z','x'}, dimensions={0} | all-to-all | bytes 262144 | tf_op jit(solution)/shard_map/all_to_all | solution.py:91
  166.8 2.0 collective-permute-start.15
  170.8 7.0 %own_gradients.1 = (f32[256,512]{1,0:T(8,128)}, bf16[256,512]{1,0:T(8,128)(2,1)}) custom-call(s32[2]{0:T(128)} %pad_add_fusion.d_ref, s32[8,128]{1,0:T(8,128)} %bitcast.179, s32[8,128]{1,0:T(8,128)} %bitcast.195, f32[8,128]{1,0:T(8,128)} %convert_element_type.99.hard_ref, f32[128,128]{1,0:T(8,128)} %get-tuple-element.93.inner_ref, ...), custom_call_target="tpu_custom_call" | custom-call | flops 2000000000 | bytes 10485760 | tf_op jit(solution)/shard_map/own_gradients/pallas_call | solution.py:262
  177.8 1.8 convolution_convert_fusion
  179.9 2.5 %collective-permute-done.16 = bf16[256,2048]{1,0:T(8,128)(2,1)S(1)} collective-permute-done((bf16[256,2048]{1,0:T(8,128)(2,1)S(1)}, bf16[256,2048]{1,0:T(8,128)(2,1)S(1)}, u32[]{:S(2)}, u32[]{:S(2)}) %collective-permute-start.16) | collective-permute-done | bytes 1048608 | tf_op jit(solution)/shard_map/ppermute | solution.py:494
  183.2 1.1 collective-permute-start.17
  184.2 1.1 collective-permute-start.19
  185.3 13.6 %coefficients.1 = (bf16[2048,128]{1,0:T(8,128)(2,1)}, bf16[128,4096]{1,0:T(8,128)(2,1)}) custom-call(s32[1]{0:T(128)} %bitcast.39.core_ref, bf16[8,32,56,128]{3,2,1,0:T(8,128)(2,1)} %bitcast.171, bf16[32,32,128]{2,1,0:T(8,128)(2,1)} %pad_maximum_fusion.5.late_ref.whole_ref, bf16[8,32,56,128]{3,2,1,0:T(8,128)(2,1)} %bitcast.172, ...), custom_call_target="tpu_custom_call" | custom-call | flops 10000000000 | bytes 8388608 | tf_op jit(solution)/shard_map/coefficients/pallas_call | solution.py:178
  198.9 1.0 collective-permute-start.20
  200.5 0.9 fusion.10
  201.8 1.1 pad_maximum_fusion.2.left_ref
  203.4 1.0 copy-done.9
  204.3 6.6 %final_product.1 = f32[128,512]{1,0:T(8,128)} custom-call(s32[1]{0:T(128)} %bitcast.24.x_ref, bf16[4096,128]{1,0:T(8,128)(2,1)} %pad_maximum_fusion.2.left_ref, bf16[128,4096]{1,0:T(8,128)(2,1)} %get-tuple-element.19.near_ref, bf16[128,4096]{1,0:T(8,128)(2,1)} %copy-done.9, f32[1,512]{1,0:T(1,128)} %bitcast.194, ...), custom_call_target="tpu_custom_call" | custom-call | flops 2000000000 | bytes 12582912 | tf_op jit(solution)/shard_map/final_product/pallas_call | solution.py:317
  (180 shorter events, 22.6 us)
Async XLA Ops:
  7.2 66.2 %all-gather.9.cloned.1.call-start = ((), (), s32[]{:S(2)}) async-start(), calls=%async_computation.4 | async-start | bytes 1179648 | tf_op jit(solution)/shard_map/all_gather | solution.py:364
  8.2 6.2 %collective-permute-start.2 = (bf16[128,512]{1,0:T(8,128)(2,1)S(1)}, bf16[128,512]{1,0:T(8,128)(2,1)S(1)}, u32[]{:S(2)}, u32[]{:S(2)}) collective-permute-start(bf16[128,512]{1,0:T(8,128)(2,1)S(1)} %get-tuple-element.78), channel_id=1, source_target_pairs={{0,4},{2,6},{4,0},{6,2},{1,5},{3,7},{5,1},{7,3},{8,12},{10,14},{12... | collective-permute-start | bytes 393224 | tf_op jit(solution)/shard_map/ppermute | solution.py:355
  12.0 6.1 %collective-permute-start.1 = (bf16[128,512]{1,0:T(8,128)(2,1)S(1)}, bf16[128,512]{1,0:T(8,128)(2,1)S(1)}, u32[]{:S(2)}, u32[]{:S(2)}) collective-permute-start(bf16[128,512]{1,0:T(8,128)(2,1)S(1)} %get-tuple-element.78), channel_id=1, source_target_pairs={{0,6},{2,0},{4,2},{6,4},{1,7},{3,1},{5,3},{7,5},{8,14},{10,8},{12,... | collective-permute-start | bytes 393224 | tf_op jit(solution)/shard_map/ppermute | solution.py:355
  12.8 7.2 %collective-permute-start = (bf16[128,512]{1,0:T(8,128)(2,1)S(1)}, bf16[128,512]{1,0:T(8,128)(2,1)S(1)}, u32[]{:S(2)}, u32[]{:S(2)}) collective-permute-start(bf16[128,512]{1,0:T(8,128)(2,1)S(1)} %get-tuple-element.78), channel_id=1, source_target_pairs={{0,2},{2,4},{4,6},{6,0},{1,3},{3,5},{5,7},{7,1},{8,10},{10,12},{12... | collective-permute-start | bytes 393224 | tf_op jit(solution)/shard_map/ppermute | solution.py:355
  20.1 3.6 %copy-start.11 = (bf16[128,2048]{1,0:T(8,128)(2,1)}, bf16[128,2048]{1,0:T(8,128)(2,1)S(1)}, u32[]{:S(2)}) copy-start(bf16[128,2048]{1,0:T(8,128)(2,1)S(1)} %pad_maximum_fusion.3) | copy-start | bytes 1572868
  20.1 4.2 %collective-permute-start.3 = (bf16[128,2048]{1,0:T(8,128)(2,1)S(1)}, bf16[128,2048]{1,0:T(8,128)(2,1)S(1)}, u32[]{:S(2)}, u32[]{:S(2)}) collective-permute-start(bf16[128,2048]{1,0:T(8,128)(2,1)S(1)} %pad_maximum_fusion.3), channel_id=1, source_target_pairs={{0,1},{1,0},{2,3},{3,2},{4,5},{5,4},{6,7},{7,6},{8,9},{9,8},{10,11... | collective-permute-start | bytes 1572872 | tf_op jit(solution)/shard_map/ppermute | solution.py:357
  24.2 2.9 %copy-start = (bf16[4,1,512,512]{3,2,1,0:T(8,128)(2,1)}, bf16[4,1,512,512]{3,2,1,0:T(8,128)(2,1)S(1)}, u32[]{:S(2)}) copy-start(bf16[4,1,512,512]{3,2,1,0:T(8,128)(2,1)S(1)} %get-tuple-element.106) | copy-start | bytes 6291460
  24.2 1.1 copy-start.17
  24.2 1.1 copy-start.20
  24.3 2.9 %copy-start.12 = (bf16[128,2048]{1,0:T(8,128)(2,1)}, bf16[128,2048]{1,0:T(8,128)(2,1)S(1)}, u32[]{:S(2)}) copy-start(bf16[128,2048]{1,0:T(8,128)(2,1)S(1)} %collective-permute-done.3) | copy-start | bytes 1572868
  27.2 6.7 %collective-permute-start.4 = (bf16[128,512]{1,0:T(8,128)(2,1)S(1)}, bf16[128,512]{1,0:T(8,128)(2,1)S(1)}, u32[]{:S(2)}, u32[]{:S(2)}) collective-permute-start(bf16[128,512]{1,0:T(8,128)(2,1)S(1)} %get-tuple-element.12), channel_id=1, source_target_pairs={{0,2},{2,4},{4,6},{6,0},{1,3},{3,5},{5,7},{7,1},{8,10},{10,12},{12... | collective-permute-start | bytes 393224 | tf_op jit(solution)/shard_map/ppermute | solution.py:355
  27.2 9.4 %collective-permute-start.6 = (bf16[128,512]{1,0:T(8,128)(2,1)S(1)}, bf16[128,512]{1,0:T(8,128)(2,1)S(1)}, u32[]{:S(2)}, u32[]{:S(2)}) collective-permute-start(bf16[128,512]{1,0:T(8,128)(2,1)S(1)} %get-tuple-element.12), channel_id=1, source_target_pairs={{0,4},{2,6},{4,0},{6,2},{1,5},{3,7},{5,1},{7,3},{8,12},{10,14},{12... | collective-permute-start | bytes 393224 | tf_op jit(solution)/shard_map/ppermute | solution.py:355
  29.4 7.1 %collective-permute-start.5 = (bf16[128,512]{1,0:T(8,128)(2,1)S(1)}, bf16[128,512]{1,0:T(8,128)(2,1)S(1)}, u32[]{:S(2)}, u32[]{:S(2)}) collective-permute-start(bf16[128,512]{1,0:T(8,128)(2,1)S(1)} %get-tuple-element.12), channel_id=1, source_target_pairs={{0,6},{2,0},{4,2},{6,4},{1,7},{3,1},{5,3},{7,5},{8,14},{10,8},{12,... | collective-permute-start | bytes 393224 | tf_op jit(solution)/shard_map/ppermute | solution.py:355
  36.6 2.8 %collective-permute-start.7 = (bf16[128,2048]{1,0:T(8,128)(2,1)S(1)}, bf16[128,2048]{1,0:T(8,128)(2,1)S(1)}, u32[]{:S(2)}, u32[]{:S(2)}) collective-permute-start(bf16[128,2048]{1,0:T(8,128)(2,1)S(1)} %constant_dynamic-update-slice_fusion), channel_id=1, source_target_pairs={{0,1},{1,0},{2,3},{3,2},{4,5},{5,4},{6,7},{7,6},{8,9},{9,8},{10,11... | collective-permute-start | bytes 1572872 | tf_op jit(solution)/shard_map/ppermute | solution.py:357
  37.9 132.9 %all-gather.7.cloned.1.call-start = ((), (), s32[]{:S(2)}) async-start(), calls=%async_computation.3 | async-start | bytes 4718592 | tf_op jit(solution)/shard_map/all_gather | solution.py:370
  37.9 2.7 %copy-start.1 = (bf16[4,1,512,512]{3,2,1,0:T(8,128)(2,1)S(1)}, bf16[4,1,512,512]{3,2,1,0:T(8,128)(2,1)}, u32[]{:S(2)}) copy-start(bf16[4,1,512,512]{3,2,1,0:T(8,128)(2,1)} %copy-done) | copy-start | bytes 6291460
  41.2 13.3 %copy-start.4 = (f32[128,512]{1,0:T(8,128)}, f32[128,512]{1,0:T(8,128)S(1)}, u32[]{:S(2)}) copy-start(f32[128,512]{1,0:T(8,128)S(1)} %get-tuple-element.103.sq_ref) | copy-start | bytes 786436
  41.2 10.2 %copy-start.16 = (s32[128,8]{0,1:T(8,128)S(1)}, s32[128,8]{0,1:T(8,128)}, u32[]{:S(2)}) copy-start(s32[128,8]{0,1:T(8,128)} %param.10) | copy-start | bytes 12292
  41.2 10.2 %copy-start.21 = (s32[128,8]{0,1:T(8,128)S(1)}, s32[128,8]{0,1:T(8,128)}, u32[]{:S(2)}) copy-start(s32[128,8]{0,1:T(8,128)} %param.11) | copy-start | bytes 12292
  41.3 6.1 %collective-permute-start.8 = (bf16[128,512]{1,0:T(8,128)(2,1)S(1)}, bf16[128,512]{1,0:T(8,128)(2,1)}, u32[]{:S(2)}, u32[]{:S(2)}) collective-permute-start(bf16[128,512]{1,0:T(8,128)(2,1)S(1)} %get-tuple-element.55), channel_id=1, source_target_pairs={{0,8},{8,16},{16,24},{24,0},{1,9},{9,17},{17,25},{25,1},{2,10},{10... | collective-permute-start | bytes 393224 | tf_op jit(solution)/shard_map/ppermute | solution.py:37
  41.8 8.6 %collective-permute-start.10 = (bf16[128,512]{1,0:T(8,128)(2,1)S(1)}, bf16[128,512]{1,0:T(8,128)(2,1)S(1)}, u32[]{:S(2)}, u32[]{:S(2)}) collective-permute-start(bf16[128,512]{1,0:T(8,128)(2,1)S(1)} %get-tuple-element.55), channel_id=1, source_target_pairs={{0,16},{8,24},{16,0},{24,8},{1,17},{9,25},{17,1},{25,9},{2,18},{10... | collective-permute-start | bytes 393224 | tf_op jit(solution)/shard_map/ppermute | solution.py:37
  44.2 6.2 %collective-permute-start.9 = (bf16[128,512]{1,0:T(8,128)(2,1)S(1)}, bf16[128,512]{1,0:T(8,128)(2,1)S(1)}, u32[]{:S(2)}, u32[]{:S(2)}) collective-permute-start(bf16[128,512]{1,0:T(8,128)(2,1)S(1)} %get-tuple-element.55), channel_id=1, source_target_pairs={{0,24},{8,0},{16,8},{24,16},{1,25},{9,1},{17,9},{25,17},{2,26},{10... | collective-permute-start | bytes 393224 | tf_op jit(solution)/shard_map/ppermute | solution.py:37
  54.5 1.8 copy-start.15
  54.5 2.0 copy-start.24
  56.5 44.2 %copy-start.25 = (s32[128]{0:T(128)S(1)}, s32[128]{0:T(128)}, u32[]{:S(2)}) copy-start(s32[128]{0:T(128)} %get-tuple-element.40) | copy-start | bytes 1540
  71.4 82.9 %copy-start.19 = (f32[1,128]{1,0:T(1,128)}, f32[1,128]{1,0:T(1,128)S(1)}, u32[]{:S(2)}) copy-start(f32[1,128]{1,0:T(1,128)S(1)} %get-tuple-element.92.invp_ref) | copy-start | bytes 1540
  73.4 23.7 %all-to-all-start.1 = ((bf16[32,56,128]{2,1,0:T(8,128)(2,1)}), bf16[32,56,128]{2,1,0:T(8,128)(2,1)S(1)}, u32[]{:S(2)}, u32[]{:S(2)}) async-start(bf16[32,56,128]{2,1,0:T(8,128)(2,1)} %pad_maximum_fusion.4), calls=%async_computation.1 | async-start | bytes 917504 | tf_op jit(solution)/shard_map/all_to_all | solution.py:424
  83.4 87.4 %all-gather.11.cloned.1.call-start = ((), (), s32[]{:S(2)}) async-start(), calls=%async_computation.5 | async-start | bytes 4128768 | tf_op jit(solution)/shard_map/all_gather | solution.py:426
  98.1 19.5 %collective-permute-start.12 = (bf16[8,128,512]{2,1,0:T(8,128)(2,1)}, bf16[8,128,512]{2,1,0:T(8,128)(2,1)S(1)}, u32[]{:S(2)}, u32[]{:S(2)}) collective-permute-start(bf16[8,128,512]{2,1,0:T(8,128)(2,1)} %bitcast.164), channel_id=1, source_target_pairs={{0,24},{8,0},{16,8},{24,16},{1,25},{9,1},{17,9},{25,17},{2,26},{10... | collective-permute-start | bytes 3145736 | tf_op jit(solution)/shard_map/ppermute | solution.py:46
  100.7 21.1 %collective-permute-start.11 = (bf16[8,128,512]{2,1,0:T(8,128)(2,1)}, bf16[8,128,512]{2,1,0:T(8,128)(2,1)}, u32[]{:S(2)}, u32[]{:S(2)}) collective-permute-start(bf16[8,128,512]{2,1,0:T(8,128)(2,1)} %bitcast.165), channel_id=1, source_target_pairs={{0,8},{8,16},{16,24},{24,0},{1,9},{9,17},{17,25},{25,1},{2,10},{10... | collective-permute-start | bytes 3145736 | tf_op jit(solution)/shard_map/ppermute | solution.py:45
  103.4 21.7 %copy-start.18 = (f32[32,128]{1,0:T(8,128)}, f32[32,128]{1,0:T(8,128)S(1)}, u32[]{:S(2)}) copy-start(f32[32,128]{1,0:T(8,128)S(1)} %convert_reduce_fusion.invp_ref) | copy-start | bytes 49156
  117.5 7.6 %copy-start.3 = (bf16[8,128,512]{2,1,0:T(8,128)(2,1)}, bf16[8,128,512]{2,1,0:T(8,128)(2,1)S(1)}, u32[]{:S(2)}) copy-start(bf16[8,128,512]{2,1,0:T(8,128)(2,1)S(1)} %collective-permute-done.12.p2) | copy-start | bytes 3145732
  117.6 12.0 %collective-permute-start.14 = (bf16[4,128,512]{2,1,0:T(8,128)(2,1)S(1)}, bf16[4,128,512]{2,1,0:T(8,128)(2,1)S(1)}, u32[]{:S(2)}, u32[]{:S(2)}) collective-permute-start(bf16[4,128,512]{2,1,0:T(8,128)(2,1)S(1)} %slice.63), channel_id=1, source_target_pairs={{0,24},{8,0},{16,8},{24,16},{1,25},{9,1},{17,9},{25,17},{2,26},{10... | collective-permute-start | bytes 1572872 | tf_op jit(solution)/shard_map/ppermute | solution.py:48
  122.9 10.2 %collective-permute-start.13 = (bf16[4,128,512]{2,1,0:T(8,128)(2,1)S(1)}, bf16[4,128,512]{2,1,0:T(8,128)(2,1)S(1)}, u32[]{:S(2)}, u32[]{:S(2)}) collective-permute-start(bf16[4,128,512]{2,1,0:T(8,128)(2,1)S(1)} %slice.62), channel_id=1, source_target_pairs={{0,8},{8,16},{16,24},{24,0},{1,9},{9,17},{17,25},{25,1},{2,10},{10... | collective-permute-start | bytes 1572872 | tf_op jit(solution)/shard_map/ppermute | solution.py:47
  134.9 18.4 %all-to-all-start = ((f32[8,8,128]{2,1,0:T(8,128)}), f32[8,8,128]{2,1,0:T(8,128)S(1)}, u32[]{:S(2)}, u32[]{:S(2)}) async-start(f32[8,8,128]{2,1,0:T(8,128)} %broadcast_in_dim.276), calls=%async_computation | async-start | bytes 65536 | tf_op jit(solution)/shard_map/all_to_all | solution.py:448
  154.2 16.6 %copy-start.22 = (f32[1,128]{1,0:T(1,128)}, f32[1,128]{1,0:T(1,128)S(1)}, u32[]{:S(2)}) copy-start(f32[1,128]{1,0:T(1,128)S(1)} %get-tuple-element.39.cq_ref) | copy-start | bytes 1540
  154.2 16.5 %copy-start.23 = (f32[1,128]{1,0:T(1,128)}, f32[1,128]{1,0:T(1,128)S(1)}, u32[]{:S(2)}) copy-start(f32[1,128]{1,0:T(1,128)S(1)} %get-tuple-element.37.tin_ref) | copy-start | bytes 1540
  166.8 3.2 %collective-permute-start.15 = (bf16[32,16,128]{2,1,0:T(8,128)(2,1)S(1)}, bf16[32,16,128]{2,1,0:T(8,128)(2,1)S(1)}, u32[]{:S(2)}, u32[]{:S(2)}) collective-permute-start(bf16[32,16,128]{2,1,0:T(8,128)(2,1)S(1)} %all_to_all.15), channel_id=1, source_target_pairs={{0,1},{1,0},{2,3},{3,2},{4,5},{5,4},{6,7},{7,6},{8,9},{9,8},{10,11... | collective-permute-start | bytes 393224 | tf_op jit(solution)/shard_map/ppermute | solution.py:479
  177.7 4.6 %copy-start.2 = (bf16[4,1,512,512]{3,2,1,0:T(8,128)(2,1)S(1)}, bf16[4,1,512,512]{3,2,1,0:T(8,128)(2,1)}, u32[]{:S(2)}) copy-start(bf16[4,1,512,512]{3,2,1,0:T(8,128)(2,1)} %copy-done) | copy-start | bytes 6291460
  177.8 4.6 %copy-start.10 = (bf16[256,512]{1,0:T(8,128)(2,1)S(1)}, bf16[256,512]{1,0:T(8,128)(2,1)}, u32[]{:S(2)}) copy-start(bf16[256,512]{1,0:T(8,128)(2,1)} %get-tuple-element.16) | copy-start | bytes 786436
  179.6 2.7 %collective-permute-start.16 = (bf16[256,2048]{1,0:T(8,128)(2,1)S(1)}, bf16[256,2048]{1,0:T(8,128)(2,1)S(1)}, u32[]{:S(2)}, u32[]{:S(2)}) collective-permute-start(bf16[256,2048]{1,0:T(8,128)(2,1)S(1)} %convolution_convert_fusion), channel_id=1, source_target_pairs={{0,1},{1,0},{2,3},{3,2},{4,5},{5,4},{6,7},{7,6},{8,9},{9,8},{10,11... | collective-permute-start | bytes 3145736 | tf_op jit(solution)/shard_map/ppermute | solution.py:494
  183.2 17.3 %collective-permute-start.17 = (bf16[256,512]{1,0:T(8,128)(2,1)S(1)}, bf16[256,512]{1,0:T(8,128)(2,1)S(1)}, u32[]{:S(2)}, u32[]{:S(2)}) collective-permute-start(bf16[256,512]{1,0:T(8,128)(2,1)S(1)} %get-tuple-element.66), channel_id=1, source_target_pairs={{0,6},{2,0},{4,2},{6,4},{1,7},{3,1},{5,3},{7,5},{8,14},{10,8},{12,... | collective-permute-start | bytes 786440 | tf_op jit(solution)/shard_map/ppermute | solution.py:499
  184.2 16.3 %collective-permute-start.19 = (bf16[256,512]{1,0:T(8,128)(2,1)S(1)}, bf16[256,512]{1,0:T(8,128)(2,1)S(1)}, u32[]{:S(2)}, u32[]{:S(2)}) collective-permute-start(bf16[256,512]{1,0:T(8,128)(2,1)S(1)} %get-tuple-element.67), channel_id=1, source_target_pairs={{0,4},{2,6},{4,0},{6,2},{1,5},{3,7},{5,1},{7,3},{8,12},{10,14},{12... | collective-permute-start | bytes 786440 | tf_op jit(solution)/shard_map/ppermute | solution.py:499
  185.3 15.2 %collective-permute-start.18 = (bf16[256,512]{1,0:T(8,128)(2,1)S(1)}, bf16[256,512]{1,0:T(8,128)(2,1)S(1)}, u32[]{:S(2)}, u32[]{:S(2)}) collective-permute-start(bf16[256,512]{1,0:T(8,128)(2,1)S(1)} %get-tuple-element.68), channel_id=1, source_target_pairs={{0,2},{2,4},{4,6},{6,0},{1,3},{3,5},{5,7},{7,1},{8,10},{10,12},{12... | collective-permute-start | bytes 786440 | tf_op jit(solution)/shard_map/ppermute | solution.py:499
  198.9 2.8 %copy-start.14 = (bf16[2048,128]{1,0:T(8,128)(2,1)S(1)}, bf16[2048,128]{1,0:T(8,128)(2,1)}, u32[]{:S(2)}) copy-start(bf16[2048,128]{1,0:T(8,128)(2,1)} %get-tuple-element.18) | copy-start | bytes 1572868
  198.9 2.8 %collective-permute-start.20 = (bf16[2048,128]{1,0:T(8,128)(2,1)}, bf16[2048,128]{1,0:T(8,128)(2,1)S(1)}, u32[]{:S(2)}, u32[]{:S(2)}) collective-permute-start(bf16[2048,128]{1,0:T(8,128)(2,1)} %get-tuple-element.18), channel_id=1, source_target_pairs={{0,1},{1,0},{2,3},{3,2},{4,5},{5,4},{6,7},{7,6},{8,9},{9,8},{10,11... | collective-permute-start | bytes 1572872 | tf_op jit(solution)/shard_map/ppermute | solution.py:503
  200.5 2.9 %collective-permute-start.21 = (bf16[128,4096]{1,0:T(8,128)(2,1)}, bf16[128,4096]{1,0:T(8,128)(2,1)S(1)}, u32[]{:S(2)}, u32[]{:S(2)}) collective-permute-start(bf16[128,4096]{1,0:T(8,128)(2,1)} %get-tuple-element.19.near_ref), channel_id=1, source_target_pairs={{0,1},{1,0},{2,3},{3,2},{4,5},{5,4},{6,7},{7,6},{8,9},{9,8},{10,11... | collective-permute-start | bytes 3145736 | tf_op jit(solution)/shard_map/ppermute | solution.py:504
  203.4 1.0 copy-start.9
  (5 other events, 4.0 us)
Sparse Core Ops, SparseCore 0:
  38.0 35.3 all-gather.8
  75.2 61.7 all-gather.6
  139.4 31.0 all-gather.10
where the time goes:
time: 218 us; the launch traced here: 217 us
  waiting for transfers between devices  60.6 us (28%)
  starting transfers between devices  50.6 us (23%)
  blocking collectives  27.1 us (12%)
  Pallas kernels  27.1 us (12%)
  between operations  14.7 us (7%)
  local copies, waits for them, and re-layouts  13.9 us (6%)
  other arithmetic  13 us (6%)
  matrix products  10.4 us (5%)
    all_gather x1, blocking collectives, body(): total = jnp.sum(lax.all_gather(part, MP, axis=0), axis=0)  14.7 us
    ppermute x1, waiting for transfers between devices, pieces_x(): right = lax.ppermute(line, 'x', shifted(NX, -1))  14.1 us
    all_to_all x1, starting transfers between devices, body(): raw = jnp.sum(lax.all_to_all(copies, MP, 0, 0, tiled=True), axis=0)  13.7 us
    pallas_call x1, Pallas kernels, coefficients(): pl.pallas_call(coef_kernel, grid=(ALL_ROWS // TILE,), in_specs=[pl.BlockS...  13.6 us
    all_to_all x1, waiting for transfers between devices, body(): share = lax.all_to_all(share, DP, 0, 0, tiled=True)  13.5 us
    ppermute x6, waiting for transfers between devices, project(): lax.ppermute(block, 'y', shifted(NY, s))  12.6 us
    all_to_all x1, blocking collectives, spread_dp(): return lax.all_to_all(copies, DP, 0, 0, tiled=True)  12.4 us
    all_to_all x1, starting transfers between devices, body(): share = lax.all_to_all(share, DP, 0, 0, tiled=True)  10 us
  transfers between devices with their start and end apart: 27, of which 17 were waited for; matrix products, arithmetic and copies ran while one was open for 12% of the time, Pallas kernels for 6%

commit v1 on v0

--- a/solution.py
+++ b/solution.py
@@ -202,7 +202,7 @@
     )(core.reshape(1), shares, late, shares, shares, shares, invp, late)
 
 def own_kernel(
-    d_ref, owner_ref, row_ref, hard_ref, inner_ref, index_ref, late_ref, sq_ref, sp_ref,
+    d_ref, owner_ref, row_ref, hard_ref, inner_ref, came_ref, sq_ref, sp_ref,
     gain_ref, cq_ref, tin_ref, invp_ref, q_ref, p0, p1, p2, p3, p4, stream_ref, rounded_ref,
     acc_q, acc_p, acc_t,
 ):
@@ -227,12 +227,9 @@
         hard = down(jnp.where(hit, hard_ref[...], 0.0))
         tall.append((jnp.where(row_of == named, hard, 0.0) + inner).astype(BF16))
         inner = jnp.where(plane * NX + n == d, inner_ref[...], 0.0)
-        owners, rows = index_rows(index_ref, g)
-        hard_k, carried_k = late_rows(late_ref, g)[:2]
-        hit = owners == d
-        named = row_of == down(jnp.where(hit, rows + 1, 0)) - 1
-        hard = down(jnp.where(hit, hard_k, 0.0))
-        moved = down(jnp.where(hit, hard_k * carried_k, 0.0))
+        came = came_ref[g].astype(F32)
+        named = row_of == came[0:1].astype(jnp.int32)
+        hard, moved = came[1:2], came[2:3] + came[3:4]
         wide.append((jnp.where(named, hard, 0.0) + inner).astype(BF16))
         acc_t[...] += jnp.where(named, moved, 0.0)
     acc_q[...] += lax.dot_general(
@@ -254,7 +251,7 @@
         rounded_ref[ROWS:, :] = grad_p.astype(BF16)
 
 
-def own_gradients(at, owner, row, hard, inner, shares, late, sq, sp, gain, cq, tin, invp, q, p):
+def own_gradients(at, owner, row, hard, inner, came, sq, sp, gain, cq, tin, invp, q, p):
     full = lambda a: pl.BlockSpec(a.shape, lambda t: (0,) * a.ndim)
     size = DEEP * NX
     tall = pl.BlockSpec((size * ROWS, FEATURES), lambda t: (t, 0))
@@ -264,7 +261,7 @@
         grid=(NZ // DEEP,),
         in_specs=[pl.BlockSpec(memory_space=pltpu.SMEM)]
         + [full(a) for a in (owner, row, hard, inner)]
-        + [shares_spec(size, 6, 8), pl.BlockSpec((size, LATE, ROWS), lambda t: (t, 0, 0))]
+        + [pl.BlockSpec((size, 8, ROWS), lambda t: (t, 2, 0))]
         + [full(a) for a in (sq, sp, gain, cq, tin, invp)]
         + [tall]
         + piece_specs(),
@@ -283,7 +280,7 @@
             flops=2 * 10**9, bytes_accessed=10 * 2**20, transcendentals=0
         ),
         name="own_gradients",
-    )(at, owner, row, hard, inner, shares, late, sq, sp, gain, cq, tin, invp, q, *p)
+    )(at, owner, row, hard, inner, came, sq, sp, gain, cq, tin, invp, q, *p)
 
 
 def final_kernel(
@@ -351,32 +348,33 @@
 
     proj_mine, proj_other = by_core(core), by_core(1 - core)
 
-    def project(block, kind):
-        parts = [block] + [lax.ppermute(block, "y", shifted(NY, s)) for s in STEPS_Y[1:]]
-        near = jnp.concatenate(parts, axis=1)
-        far = lax.ppermute(near, "core", shifted(NC, 1))
-        hidden = jnp.dot(near, proj_mine, preferred_element_type=F32)
-        hidden = hidden + jnp.dot(far, proj_other, preferred_element_type=F32)
-        scaled = (hidden + stream[kind].astype(F32)) * gain[None, :]
-        return (near, far), scaled, scaled.astype(BF16)
-
-    pair_p, scaled_p, passages = project(attn[1], 1)
+    block = attn.reshape(2 * ROWS, FEATURES)
+    parts = [block] + [lax.ppermute(block, "y", shifted(NY, s)) for s in STEPS_Y[1:]]
+    near = jnp.concatenate(parts, axis=1)
+    far = lax.ppermute(near, "core", shifted(NC, 1))
+    hidden = jnp.dot(near, proj_mine, preferred_element_type=F32)
+    hidden = hidden + jnp.dot(far, proj_other, preferred_element_type=F32)
+    scaled = (hidden + stream.reshape(2 * ROWS, FEATURES).astype(F32)) * gain[None, :]
+    scaled_q, scaled_p = scaled[:ROWS], scaled[ROWS:]
+    queries, passages = scaled_q.astype(BF16), scaled_p.astype(BF16)
+
     p_line = lax.all_gather(passages, "z", axis=0)
     p_pieces = pieces_x(p_line)
 
-    attn_q, _ = lax.optimization_barrier((attn[0], passages))
-    pair_q, scaled_q, queries = project(attn_q, 0)
     column = gather_x(queries).reshape(NX * ROWS, FEATURES)
     q_all = lax.all_gather(column, "z", axis=0, tiled=True)
 
-    def some_rows(pair):
-        cut = [lax.dynamic_slice_in_dim(v, m * 16, 16, 0).reshape(16, NY, FEATURES) for v in pair]
+    def some_rows(kind):
+        first = kind * ROWS + m * 16
+        cut = [
+            lax.dynamic_slice_in_dim(v, first, 16, 0).reshape(16, NY, FEATURES) for v in (near, far)
+        ]
         both = jnp.stack([jnp.where(core == 0, cut[c], cut[1 - c]) for c in range(NC)])
         at = lambda a: jnp.where((y - a) % NY == 3, 2, jnp.where((y - a) % NY == 2, 3, (y - a) % NY))
         rows = [lax.dynamic_index_in_dim(both, at(a), 2, keepdims=False) for a in range(NY)]
         return jnp.stack(rows)
 
-    mine = jnp.stack([some_rows(pair_q), some_rows(pair_p)])
+    mine = jnp.stack([some_rows(0), some_rows(1)])
     mine = mine.reshape(2, NZ, 16, NX, ROWS).transpose(1, 3, 0, 2, 4).reshape(N_DP, 32, ROWS)
 
     owner, row = neg_owner.T, neg_row.T
@@ -422,11 +420,13 @@
     share = jnp.concatenate([mine, jnp.broadcast_to(share[None], (N_DP, 24, ROWS))], axis=1)
     share, _ = lax.optimization_barrier((share, p_line))
     share = lax.all_to_all(share, DP, 0, 0, tiled=True)
-    invp_all = jnp.sum(share[:, 50:53].astype(F32), axis=1)
     shares = lax.all_gather(share, MP, axis=0)
 
     row_iota = jnp.arange(ROWS, dtype=jnp.int32)
     named = rows_own[:, None, :] == row_iota[None, :, None]
+    *close, share = lax.optimization_barrier(p_pieces[:3] + (share,))
+    p_pieces = tuple(close) + p_pieces[3:]
+    invp_all = jnp.sum(share[:, 50:53].astype(F32), axis=1)
     invp_named = jnp.sum(jnp.where(named, invp_all[:, :, None], 0.0), axis=1)
     raw_hard = jnp.zeros((NEG, ROWS), F32)
     for piece, s, first in zip(p_pieces, (0, 1, 3, 2, 2), (0, 0, 0, 0, NZ // 2)):
@@ -475,7 +475,14 @@
     late = [hard] + pieces(carried) + [jnp.stack(pieces(factor) + [diag] + pieces(cq) + pieces(tin) + [diag])]
     late = jnp.concatenate([v.astype(BF16) for v in late], axis=0)
     late_half = lax.dynamic_slice_in_dim(late, core * (LATE // 2), LATE // 2, 0)
-    late_half = spread_dp(late_half)
+    sums = pieces(dense(owner, hard * carried, 0.0))
+    named_there = [rows_own.astype(F32), dense(owner, hard, 0.0)] + sums
+    named_there = jnp.stack([v.astype(BF16) for v in named_there] + [jnp.zeros((N_DP, ROWS), BF16)] * 4, axis=1)
+    came = jnp.concatenate(
+        [jnp.broadcast_to(late_half[None], (N_DP, LATE // 2, ROWS)), named_there], axis=1
+    )
+    came = lax.all_to_all(came, DP, 0, 0, tiled=True)
+    late_half = came[:, : LATE // 2]
     late_other = lax.ppermute(late_half, "core", shifted(NC, 1))
     late_all = jnp.concatenate(
         [jnp.where(core == 0, late_half, late_other), jnp.where(core == 0, late_other, late_half)],
@@ -484,7 +491,7 @@
 
     line = lambda v: v.reshape(1, -1)
     grad_stream, rounded = own_gradients(
-        jnp.stack([d, x]), owner, row, hard, inner, shares, late_all, scaled_q, scaled_p,
+        jnp.stack([d, x]), owner, row, hard, inner, came, scaled_q, scaled_p,
         line(gain), line(cq), line(tin), line(inv_p), q_all, p_pieces,
     )
 

time: 218 us -> 206 us (0.945)
  blocking collectives: 27.1 us -> 14.1 us
  waiting for transfers between devices: 60.6 us -> 48.3 us
  other arithmetic: 13 us -> 18.8 us
  starting transfers between devices: 50.6 us -> 55.5 us
    ppermute x1, waiting for transfers between devices: 14.1 us -> 0.01 us  [pieces_x(): right = lax.ppermute(line, 'x', shifted(NX, -1))]
    all_to_all x1 -> x0, blocking collectives: 12.4 us -> none  [spread_dp(): return lax.all_to_all(copies, DP, 0, 0, tiled=True)]
    all_to_all x0 -> x1, starting transfers between devices: none -> 9.6 us  [body(): came = lax.all_to_all(came, DP, 0, 0, tiled=True)]
    all_to_all x0 -> x1, waiting for transfers between devices: none -> 9.32 us  [body(): came = lax.all_to_all(came, DP, 0, 0, tiled=True)]
    ppermute x1, waiting for transfers between devices: 4.32 us -> 0.01 us  [pieces_x(): high = lax.ppermute(right[NZ // 2:], 'x', shifted(NX, -1))]
    ppermute x8 -> x4, starting transfers between devices: 11 us -> 6.8 us  [the longest x3 5.3 us: body(): lax.ppermute(block, 'y', shifted(NY, s))]
    ppermute x8 -> x4, waiting for transfers between devices: 14 us -> 10.7 us  [the longest x3 10.7 us: body(): lax.ppermute(block, 'y', shifted(NY, s))]
    ppermute x1, waiting for transfers between devices: 0.01 us -> 2.51 us  [body(): late_other = lax.ppermute(late_half, 'core', shifted(NC, 1))]
  transfers between devices with their start and end apart: 27 -> 24, of which waited for: 17 -> 11; matrix products, arithmetic and copies ran while one was open for 12% -> 17% of each run, Pallas kernels for 6% -> 10%
where the time goes in v1:
time: 206 us; the launch traced here: 204 us
  starting transfers between devices  55.5 us (27%)
  waiting for transfers between devices  48.3 us (23%)
  Pallas kernels  27.1 us (13%)
  other arithmetic  18.8 us (9%)
  between operations  14.9 us (7%)
  local copies, waits for them, and re-layouts  14.5 us (7%)
  blocking collectives  14.1 us (7%)
  matrix products  10.7 us (5%)
    all_gather x1, blocking collectives, body(): total = jnp.sum(lax.all_gather(part, MP, axis=0), axis=0)  14.1 us
    pallas_call x1, Pallas kernels, coefficients(): pl.pallas_call(coef_kernel, grid=(ALL_ROWS // TILE,), in_specs=[pl.BlockS...  13.6 us
    all_to_all x1, starting transfers between devices, body(): raw = jnp.sum(lax.all_to_all(copies, MP, 0, 0, tiled=True), axis=0)  12.5 us
    all_to_all x1, waiting for transfers between devices, body(): share = lax.all_to_all(share, DP, 0, 0, tiled=True)  12.4 us
    ppermute x3, waiting for transfers between devices, body(): lax.ppermute(block, 'y', shifted(NY, s))  10.7 us
    all_to_all x1, starting transfers between devices, body(): came = lax.all_to_all(came, DP, 0, 0, tiled=True)  9.6 us
    all_to_all x1, waiting for transfers between devices, body(): came = lax.all_to_all(came, DP, 0, 0, tiled=True)  9.32 us
    all_to_all x1, starting transfers between devices, body(): share = lax.all_to_all(share, DP, 0, 0, tiled=True)  8.2 us
  transfers between devices with their start and end apart: 24, of which 11 were waited for; matrix products, arithmetic and copies ran while one was open for 17% of the time, Pallas kernels for 10%

profile of v1, /device:TPU:1, one launch (start us, length us, event | category | flops | bytes accessed | tf_op | source)
XLA Modules:
  0.0 204.0 jit_solution(9056043313950010606)
XLA Ops:
  7.2 3.8 %collective-permute-start.2 = (bf16[256,512]{1,0:T(8,128)(2,1)}, bf16[256,512]{1,0:T(8,128)(2,1)S(1)}, u32[]{:S(2)}, u32[]{:S(2)}) collective-permute-start(bf16[256,512]{1,0:T(8,128)(2,1)} %bitcast.178), channel_id=1, source_target_pairs={{0,4},{2,6},{4,0},{6,2},{1,5},{3,7},{5,1},{7,3},{8,12},{10,14},{12... | collective-permute-start | bytes 786440 | tf_op jit(solution)/shard_map/ppermute | solution.py:352
  11.0 0.8 collective-permute-start.1
  12.5 3.9 %collective-permute-done.2 = bf16[256,512]{1,0:T(8,128)(2,1)S(1)} collective-permute-done((bf16[256,512]{1,0:T(8,128)(2,1)}, bf16[256,512]{1,0:T(8,128)(2,1)S(1)}, u32[]{:S(2)}, u32[]{:S(2)}) %collective-permute-start.2) | collective-permute-done | bytes 262176 | tf_op jit(solution)/shard_map/ppermute | solution.py:352
  16.4 6.7 %collective-permute-done.1 = bf16[256,512]{1,0:T(8,128)(2,1)S(1)} collective-permute-done((bf16[256,512]{1,0:T(8,128)(2,1)}, bf16[256,512]{1,0:T(8,128)(2,1)S(1)}, u32[]{:S(2)}, u32[]{:S(2)}) %collective-permute-start.1) | collective-permute-done | bytes 262176 | tf_op jit(solution)/shard_map/ppermute | solution.py:352
  23.2 1.2 pad_maximum_fusion.2
  24.4 1.5 collective-permute-start.3
  25.9 2.4 %constant_dynamic-slice_fusion.18 = (bf16[1,1,512,512]{3,2,1,0:T(8,128)(2,1)S(1)}, bf16[1,1,512,512]{3,2,1,0:T(8,128)(2,1)S(1)}, bf16[1,1,512,512]{3,2,1,0:T(8,1...) fusion(bf16[4,2,512,512]{3,2,1,0:T(8,128)(2,1)} %bitcast.165, ...), kind=kLoop, calls=%fused_computation.131 | loop fusion | bytes 8388632 | tf_op jit(solution)/shard_map/dynamic_slice | solution.py:344
  29.0 2.7 %fusion.58 = f32[256,512]{1,0:T(8,128)S(1)} fusion(bf16[256,2048]{1,0:T(8,128)(2,1)} %collective-permute-done.3, bf16[2048,512]{1,0:T(8,128)(2,1)S(1)} %bitcast.158), kind=kOutput, calls=%fused_computation.217 | convolution fusion | flops 536870912 | bytes 3670016 | tf_op jit(solution)/shard_map/dot_general | solution.py:356
  33.4 1.3 collective-permute-start.4
  34.7 1.5 collective-permute-start.5
  36.2 1.5 collective-permute-start.6
  37.7 1.8 collective-permute-done.4
  39.6 3.7 %collective-permute-done.6 = bf16[128,512]{1,0:T(8,128)(2,1)S(1)} collective-permute-done((bf16[128,512]{1,0:T(8,128)(2,1)S(1)}, bf16[128,512]{1,0:T(8,128)(2,1)S(1)}, u32[]{:S(2)}, u32[]{:S(2)}) %collective-permute-start.6) | collective-permute-done | bytes 131104 | tf_op jit(solution)/shard_map/ppermute | solution.py:37
  43.3 0.8 copy-done.8
  49.4 1.0 broadcast_select_fusion.6
  52.0 0.8 multiply_reduce_fusion.1
  52.9 14.1 %all-gather = f32[1088,128]{1,0:T(8,128)S(1)} all-gather(f32[136,128]{1,0:T(8,128)S(1)} %maximum_maximum_fusion), channel_id=2, replica_groups=mesh['z'=8,'x'=4,'y'=4,'core'=2] {'y','core'}, dimensions={0}, use_global_device_ids=true | all-gather | bytes 626688 | tf_op jit(solution)/shard_map/all_gather | solution.py:395
  69.0 0.9 all-gather.9.cloned.1.call-done
  70.3 2.3 %collective-permute-start.8 = (bf16[8,128,512]{2,1,0:T(8,128)(2,1)}, bf16[8,128,512]{2,1,0:T(8,128)(2,1)}, u32[]{:S(2)}, u32[]{:S(2)}) collective-permute-start(bf16[8,128,512]{2,1,0:T(8,128)(2,1)} %bitcast.161), channel_id=1, source_target_pairs={{0,24},{8,0},{16,8},{24,16},{1,25},{9,1},{17,9},{25,17},{2,26},{10... | collective-permute-start | bytes 3145736 | tf_op jit(solution)/shard_map/ppermute | solution.py:46
  73.9 0.8 pad_maximum_fusion.4
  74.7 8.2 %all-to-all-start = ((bf16[32,56,128]{2,1,0:T(8,128)(2,1)}), bf16[32,56,128]{2,1,0:T(8,128)(2,1)}, u32[]{:S(2)}, u32[]{:S(2)}) async-start(bf16[32,56,128]{2,1,0:T(8,128)(2,1)} %pad_maximum_fusion.4), calls=%async_computation | async-start | bytes 917504 | tf_op jit(solution)/shard_map/all_to_all | solution.py:422
  83.7 12.4 %all-to-all-done = bf16[32,56,128]{2,1,0:T(8,128)(2,1)} async-done(((bf16[32,56,128]{2,1,0:T(8,128)(2,1)}), bf16[32,56,128]{2,1,0:T(8,128)(2,1)}, u32[]{:S(2)}, u32[]{:S(2)}) %all-to-all-start) | async-done | bytes 458784 | tf_op jit(solution)/shard_map/all_to_all | solution.py:422
  96.2 2.0 collective-permute-start.9
  98.2 1.1 slice.61
  99.3 1.2 collective-permute-start.10
  101.0 1.7 fusion.4
  103.3 0.9 convert_reduce_fusion.invp_ref
  105.0 2.1 %collective-permute-done.9.p3 = bf16[4,128,512]{2,1,0:T(8,128)(2,1)S(1)} collective-permute-done((bf16[4,128,512]{2,1,0:T(8,128)(2,1)S(1)}, bf16[4,128,512]{2,1,0:T(8,128)(2,1)S(1)}, u32[]{:S(2)}, u32[]{:S(2)}) %collective-permute-start.9) | collective-permute-done | bytes 524320 | tf_op jit(solution)/shard_map/ppermute | solution.py:47
  107.1 0.8 copy-done.6
  108.2 0.8 copy-done.7
  110.1 12.5 %all-to-all-start.1 = ((f32[8,8,128]{2,1,0:T(8,128)}), f32[8,8,128]{2,1,0:T(8,128)S(1)}, u32[]{:S(2)}, u32[]{:S(2)}) async-start(f32[8,8,128]{2,1,0:T(8,128)} %broadcast_in_dim.299), calls=%async_computation.1 | async-start | bytes 65536 | tf_op jit(solution)/shard_map/all_to_all | solution.py:448
  122.6 4.7 %all-to-all-done.1 = f32[8,8,128]{2,1,0:T(8,128)S(1)} async-done(((f32[8,8,128]{2,1,0:T(8,128)}), f32[8,8,128]{2,1,0:T(8,128)S(1)}, u32[]{:S(2)}, u32[]{:S(2)}) %all-to-all-start.1) | async-done | bytes 32800 | tf_op jit(solution)/shard_map/all_to_all | solution.py:448
  128.7 1.4 concatenate.43
  130.1 9.6 %all-to-all-start.2 = ((bf16[32,24,128]{2,1,0:T(8,128)(2,1)}), bf16[32,24,128]{2,1,0:T(8,128)(2,1)S(1)}, u32[]{:S(2)}, u32[]{:S(2)}) async-start(bf16[32,24,128]{2,1,0:T(8,128)(2,1)} %concatenate.43), calls=%async_computation.2 | async-start | bytes 393216 | tf_op jit(solution)/shard_map/all_to_all | solution.py:484
  140.3 9.3 %all-to-all-done.2.came_ref = bf16[32,24,128]{2,1,0:T(8,128)(2,1)S(1)} async-done(((bf16[32,24,128]{2,1,0:T(8,128)(2,1)}), bf16[32,24,128]{2,1,0:T(8,128)(2,1)S(1)}, u32[]{:S(2)}, u32[]{:S(2)}) %all-to-all-start.2) | async-done | bytes 196640 | tf_op jit(solution)/shard_map/all_to_all | solution.py:484
  150.3 7.0 %own_gradients.1 = (f32[256,512]{1,0:T(8,128)}, bf16[256,512]{1,0:T(8,128)(2,1)}) custom-call(s32[2]{0:T(128)} %pad_add_fusion.d_ref, s32[8,128]{1,0:T(8,128)} %bitcast.170, s32[8,128]{1,0:T(8,128)} %bitcast.192, f32[8,128]{1,0:T(8,128)} %copy-done.24, f32[128,128]{1,0:T(8,128)} %get-tuple-element.99.inner_ref, bf16[32,24,128]{2,1,0:T(8,128)(2,1)} %copy-done.4, ...), custom_call_target="tpu_custom_call" | custom-call | flops 2000000000 | bytes 10485760 | tf_op jit(solution)/shard_map/own_gradients/pallas_call | solution.py:259
  157.4 1.8 convolution_convert_fusion
  159.1 2.8 %collective-permute-start.11 = (bf16[256,2048]{1,0:T(8,128)(2,1)S(1)}, bf16[256,2048]{1,0:T(8,128)(2,1)S(1)}, u32[]{:S(2)}, u32[]{:S(2)}) collective-permute-start(bf16[256,2048]{1,0:T(8,128)(2,1)S(1)} %convolution_convert_fusion), channel_id=1, source_target_pairs={{0,1},{1,0},{2,3},{3,2},{4,5},{5,4},{6,7},{7,6},{8,9},{9,8},{10,11... | collective-permute-start | bytes 3145736 | tf_op jit(solution)/shard_map/ppermute | solution.py:501
  162.0 2.5 %collective-permute-done.15 = bf16[32,16,128]{2,1,0:T(8,128)(2,1)S(1)} collective-permute-done((bf16[32,16,128]{2,1,0:T(8,128)(2,1)S(1)}, bf16[32,16,128]{2,1,0:T(8,128)(2,1)S(1)}, u32[]{:S(2)}, u32[]{:S(2)}) %collective-permute-start.15) | collective-permute-done | bytes 131104 | tf_op jit(solution)/shard_map/ppermute | solution.py:486
  165.3 2.1 %fusion.55 = (bf16[256,2048]{1,0:T(8,128)(2,1)S(1)}, f32[256,2048]{1,0:T(8,128)}) fusion(bf16[256,2048]{1,0:T(8,128)(2,1)S(1)} %collective-permute-done.11, bf16[256,512]{1,0:T(8,128)(2,1)S(1)} %copy-done.11, bf16[2048,512]{1,0:T(8,128)(2,1)S(1)} %bitcast.157), kind=kOutput, calls=%fused_computation.214 | convolution fusion | flops 538443776 | bytes 6553600 | tf_op jit(solution)/shard_map/dot_general | solution.py:498
  167.5 1.2 collective-permute-start.14
  169.1 2.3 %collective-permute-start.12 = (bf16[256,512]{1,0:T(8,128)(2,1)S(1)}, bf16[256,512]{1,0:T(8,128)(2,1)S(1)}, u32[]{:S(2)}, u32[]{:S(2)}) collective-permute-start(bf16[256,512]{1,0:T(8,128)(2,1)S(1)} %get-tuple-element.80), channel_id=1, source_target_pairs={{0,6},{2,0},{4,2},{6,4},{1,7},{3,1},{5,3},{7,5},{8,14},{10,8},{12,... | collective-permute-start | bytes 786440 | tf_op jit(solution)/shard_map/ppermute | solution.py:506
  171.4 13.6 %coefficients.1 = (bf16[2048,128]{1,0:T(8,128)(2,1)}, bf16[128,4096]{1,0:T(8,128)(2,1)}) custom-call(s32[1]{0:T(128)} %bitcast.39.core_ref, bf16[8,32,56,128]{3,2,1,0:T(8,128)(2,1)} %bitcast.202, bf16[32,32,128]{2,1,0:T(8,128)(2,1)} %pad_maximum_fusion.5.late_ref.whole_ref, bf16[8,32,56,128]{3,2,1,0:T(8,128)(2,1)} %bitcast.203, ...), custom_call_target="tpu_custom_call" | custom-call | flops 10000000000 | bytes 8388608 | tf_op jit(solution)/shard_map/coefficients/pallas_call | solution.py:178
  185.0 1.3 collective-permute-start.16
  186.8 2.0 fusion.8
  188.8 1.0 pad_maximum_fusion.3.left_ref
  189.9 1.0 copy-done.10
  190.9 6.6 %final_product.1 = f32[128,512]{1,0:T(8,128)} custom-call(s32[1]{0:T(128)} %bitcast.22.x_ref, bf16[4096,128]{1,0:T(8,128)(2,1)} %pad_maximum_fusion.3.left_ref, bf16[128,4096]{1,0:T(8,128)(2,1)} %get-tuple-element.25.near_ref, bf16[128,4096]{1,0:T(8,128)(2,1)} %copy-done.10, f32[1,512]{1,0:T(1,128)} %bitcast.198, ...), custom_call_target="tpu_custom_call" | custom-call | flops 2000000000 | bytes 12582912 | tf_op jit(solution)/shard_map/final_product/pallas_call | solution.py:314
  (226 shorter events, 21.6 us)
Async XLA Ops:
  7.2 62.7 %all-gather.9.cloned.1.call-start = ((), (), s32[]{:S(2)}) async-start(), calls=%async_computation.4 | async-start | bytes 1179648 | tf_op jit(solution)/shard_map/all_gather | solution.py:361
  7.2 9.2 %collective-permute-start.2 = (bf16[256,512]{1,0:T(8,128)(2,1)}, bf16[256,512]{1,0:T(8,128)(2,1)S(1)}, u32[]{:S(2)}, u32[]{:S(2)}) collective-permute-start(bf16[256,512]{1,0:T(8,128)(2,1)} %bitcast.178), channel_id=1, source_target_pairs={{0,4},{2,6},{4,0},{6,2},{1,5},{3,7},{5,1},{7,3},{8,12},{10,14},{12... | collective-permute-start | bytes 786440 | tf_op jit(solution)/shard_map/ppermute | solution.py:352
  11.0 12.1 %collective-permute-start.1 = (bf16[256,512]{1,0:T(8,128)(2,1)}, bf16[256,512]{1,0:T(8,128)(2,1)S(1)}, u32[]{:S(2)}, u32[]{:S(2)}) collective-permute-start(bf16[256,512]{1,0:T(8,128)(2,1)} %bitcast.179), channel_id=1, source_target_pairs={{0,6},{2,0},{4,2},{6,4},{1,7},{3,1},{5,3},{7,5},{8,14},{10,8},{12,... | collective-permute-start | bytes 786440 | tf_op jit(solution)/shard_map/ppermute | solution.py:352
  11.8 11.4 %collective-permute-start = (bf16[256,512]{1,0:T(8,128)(2,1)}, bf16[256,512]{1,0:T(8,128)(2,1)S(1)}, u32[]{:S(2)}, u32[]{:S(2)}) collective-permute-start(bf16[256,512]{1,0:T(8,128)(2,1)} %bitcast.180), channel_id=1, source_target_pairs={{0,2},{2,4},{4,6},{6,0},{1,3},{3,5},{5,7},{7,1},{8,10},{10,12},{12... | collective-permute-start | bytes 786440 | tf_op jit(solution)/shard_map/ppermute | solution.py:352
  24.4 4.6 %collective-permute-start.3 = (bf16[256,2048]{1,0:T(8,128)(2,1)S(1)}, bf16[256,2048]{1,0:T(8,128)(2,1)}, u32[]{:S(2)}, u32[]{:S(2)}) collective-permute-start(bf16[256,2048]{1,0:T(8,128)(2,1)S(1)} %pad_maximum_fusion.2), channel_id=1, source_target_pairs={{0,1},{1,0},{2,3},{3,2},{4,5},{5,4},{6,7},{7,6},{8,9},{9,8},{10,11... | collective-permute-start | bytes 3145736 | tf_op jit(solution)/shard_map/ppermute | solution.py:354
  32.5 11.7 %copy-start.15 = (s32[128,8]{0,1:T(8,128)S(1)}, s32[128,8]{0,1:T(8,128)}, u32[]{:S(2)}) copy-start(s32[128,8]{0,1:T(8,128)} %param.10) | copy-start | bytes 12292
  32.5 11.7 %copy-start.25 = (s32[128,8]{0,1:T(8,128)S(1)}, s32[128,8]{0,1:T(8,128)}, u32[]{:S(2)}) copy-start(s32[128,8]{0,1:T(8,128)} %param.11) | copy-start | bytes 12292
  33.3 116.4 %all-gather.7.cloned.1.call-start = ((), (), s32[]{:S(2)}) async-start(), calls=%async_computation.3 | async-start | bytes 4718592 | tf_op jit(solution)/shard_map/all_gather | solution.py:365
  33.4 18.4 %copy-start.13 = (bf16[128,512]{1,0:T(8,128)(2,1)}, bf16[128,512]{1,0:T(8,128)(2,1)S(1)}, u32[]{:S(2)}) copy-start(bf16[128,512]{1,0:T(8,128)(2,1)S(1)} %get-tuple-element.65) | copy-start | bytes 393220
  33.4 6.1 %collective-permute-start.4 = (bf16[128,512]{1,0:T(8,128)(2,1)S(1)}, bf16[128,512]{1,0:T(8,128)(2,1)S(1)}, u32[]{:S(2)}, u32[]{:S(2)}) collective-permute-start(bf16[128,512]{1,0:T(8,128)(2,1)S(1)} %get-tuple-element.65), channel_id=1, source_target_pairs={{0,8},{8,16},{16,24},{24,0},{1,9},{9,17},{17,25},{25,1},{2,10},{10... | collective-permute-start | bytes 393224 | tf_op jit(solution)/shard_map/ppermute | solution.py:37
  34.7 4.8 %collective-permute-start.5 = (bf16[128,512]{1,0:T(8,128)(2,1)S(1)}, bf16[128,512]{1,0:T(8,128)(2,1)S(1)}, u32[]{:S(2)}, u32[]{:S(2)}) collective-permute-start(bf16[128,512]{1,0:T(8,128)(2,1)S(1)} %get-tuple-element.65), channel_id=1, source_target_pairs={{0,24},{8,0},{16,8},{24,16},{1,25},{9,1},{17,9},{25,17},{2,26},{10... | collective-permute-start | bytes 393224 | tf_op jit(solution)/shard_map/ppermute | solution.py:37
  36.2 7.1 %collective-permute-start.6 = (bf16[128,512]{1,0:T(8,128)(2,1)S(1)}, bf16[128,512]{1,0:T(8,128)(2,1)S(1)}, u32[]{:S(2)}, u32[]{:S(2)}) collective-permute-start(bf16[128,512]{1,0:T(8,128)(2,1)S(1)} %get-tuple-element.65), channel_id=1, source_target_pairs={{0,16},{8,24},{16,0},{24,8},{1,17},{9,25},{17,1},{25,9},{2,18},{10... | collective-permute-start | bytes 393224 | tf_op jit(solution)/shard_map/ppermute | solution.py:37
  52.8 30.8 %copy-start.27 = (s32[8,128]{1,0:T(8,128)S(1)}, s32[8,128]{1,0:T(8,128)}, u32[]{:S(2)}) copy-start(s32[8,128]{1,0:T(8,128)} %get-tuple-element.32) | copy-start | bytes 12292
  52.8 30.8 %copy-start.28 = (s32[8,128]{1,0:T(8,128)S(1)}, s32[8,128]{1,0:T(8,128)}, u32[]{:S(2)}) copy-start(s32[8,128]{1,0:T(8,128)} %get-tuple-element.33) | copy-start | bytes 12292
  67.7 31.6 %copy-start.29 = (f32[128]{0:T(128)}, f32[128]{0:T(128)S(1)}, u32[]{:S(2)}) copy-start(f32[128]{0:T(128)S(1)} %get-tuple-element.98) | copy-start | bytes 1540
  67.7 60.7 %copy-start.26 = (f32[1,128]{1,0:T(1,128)}, f32[1,128]{1,0:T(1,128)S(1)}, u32[]{:S(2)}) copy-start(f32[1,128]{1,0:T(1,128)S(1)} %get-tuple-element.61.invp_ref) | copy-start | bytes 1540
  67.8 31.5 %copy-start.31 = (f32[128]{0:T(128)}, f32[128]{0:T(128)S(1)}, u32[]{:S(2)}) copy-start(f32[128]{0:T(128)S(1)} %fusion.50) | copy-start | bytes 1540
  69.9 26.2 %collective-permute-start.7 = (bf16[8,128,512]{2,1,0:T(8,128)(2,1)}, bf16[8,128,512]{2,1,0:T(8,128)(2,1)S(1)}, u32[]{:S(2)}, u32[]{:S(2)}) collective-permute-start(bf16[8,128,512]{2,1,0:T(8,128)(2,1)} %bitcast.160), channel_id=1, source_target_pairs={{0,8},{8,16},{16,24},{24,0},{1,9},{9,17},{17,25},{25,1},{2,10},{10... | collective-permute-start | bytes 3145736 | tf_op jit(solution)/shard_map/ppermute | solution.py:45
  70.3 27.9 %collective-permute-start.8 = (bf16[8,128,512]{2,1,0:T(8,128)(2,1)}, bf16[8,128,512]{2,1,0:T(8,128)(2,1)}, u32[]{:S(2)}, u32[]{:S(2)}) collective-permute-start(bf16[8,128,512]{2,1,0:T(8,128)(2,1)} %bitcast.161), channel_id=1, source_target_pairs={{0,24},{8,0},{16,8},{24,16},{1,25},{9,1},{17,9},{25,17},{2,26},{10... | collective-permute-start | bytes 3145736 | tf_op jit(solution)/shard_map/ppermute | solution.py:46
  74.7 25.8 %copy-start.14 = (bf16[128,512]{1,0:T(8,128)(2,1)S(1)}, bf16[128,512]{1,0:T(8,128)(2,1)}, u32[]{:S(2)}) copy-start(bf16[128,512]{1,0:T(8,128)(2,1)} %copy-done.13) | copy-start | bytes 393220
  74.7 21.4 %all-to-all-start = ((bf16[32,56,128]{2,1,0:T(8,128)(2,1)}), bf16[32,56,128]{2,1,0:T(8,128)(2,1)}, u32[]{:S(2)}, u32[]{:S(2)}) async-start(bf16[32,56,128]{2,1,0:T(8,128)(2,1)} %pad_maximum_fusion.4), calls=%async_computation | async-start | bytes 917504 | tf_op jit(solution)/shard_map/all_to_all | solution.py:422
  82.9 88.5 %all-gather.11.cloned.1.call-start = ((), (), s32[]{:S(2)}) async-start(), calls=%async_computation.5 | async-start | bytes 4128768 | tf_op jit(solution)/shard_map/all_gather | solution.py:423
  96.1 6.6 %copy-start.2 = (bf16[8,128,512]{2,1,0:T(8,128)(2,1)}, bf16[8,128,512]{2,1,0:T(8,128)(2,1)S(1)}, u32[]{:S(2)}) copy-start(bf16[8,128,512]{2,1,0:T(8,128)(2,1)S(1)} %collective-permute-done.7.p1) | copy-start | bytes 3145732
  96.2 11.0 %collective-permute-start.9 = (bf16[4,128,512]{2,1,0:T(8,128)(2,1)S(1)}, bf16[4,128,512]{2,1,0:T(8,128)(2,1)S(1)}, u32[]{:S(2)}, u32[]{:S(2)}) collective-permute-start(bf16[4,128,512]{2,1,0:T(8,128)(2,1)S(1)} %slice.60), channel_id=1, source_target_pairs={{0,8},{8,16},{16,24},{24,0},{1,9},{9,17},{17,25},{25,1},{2,10},{10... | collective-permute-start | bytes 1572872 | tf_op jit(solution)/shard_map/ppermute | solution.py:47
  99.3 8.9 %collective-permute-start.10 = (bf16[4,128,512]{2,1,0:T(8,128)(2,1)S(1)}, bf16[4,128,512]{2,1,0:T(8,128)(2,1)S(1)}, u32[]{:S(2)}, u32[]{:S(2)}) collective-permute-start(bf16[4,128,512]{2,1,0:T(8,128)(2,1)S(1)} %slice.61), channel_id=1, source_target_pairs={{0,24},{8,0},{16,8},{24,16},{1,25},{9,1},{17,9},{25,17},{2,26},{10... | collective-permute-start | bytes 1572872 | tf_op jit(solution)/shard_map/ppermute | solution.py:48
  101.0 6.9 %copy-start.45 = (s32[4,128]{1,0:T(4,128)S(1)}, s32[4,128]{1,0:T(4,128)}, u32[]{:S(2)}) copy-start(s32[4,128]{1,0:T(4,128)} %broadcast_add_fusion.6) | copy-start | bytes 6148
  102.7 6.7 %copy-start.47 = (s32[4]{0:T(128)S(1)}, s32[4]{0:T(128)}, u32[]{:S(2)}) copy-start(s32[4]{0:T(128)} %copy-done.46) | copy-start | bytes 52
  102.7 6.7 %copy-start.49 = (s32[4]{0:T(128)S(1)}, s32[4]{0:T(128)}, u32[]{:S(2)}) copy-start(s32[4]{0:T(128)} %copy-done.48) | copy-start | bytes 52
  102.7 24.7 %copy-start.30 = (f32[128]{0:T(128)S(1)}, f32[128]{0:T(128)}, u32[]{:S(2)}) copy-start(f32[128]{0:T(128)} %copy-done.29) | copy-start | bytes 1540
  102.7 24.7 %copy-start.32 = (f32[128]{0:T(128)S(1)}, f32[128]{0:T(128)}, u32[]{:S(2)}) copy-start(f32[128]{0:T(128)} %copy-done.31) | copy-start | bytes 1540
  102.7 24.7 %copy-start.34 = (f32[128]{0:T(128)S(1)}, f32[128]{0:T(128)}, u32[]{:S(2)}) copy-start(f32[128]{0:T(128)} %get-tuple-element.31) | copy-start | bytes 1540
  102.7 24.7 %copy-start.44 = (f32[128]{0:T(128)S(1)}, f32[128]{0:T(128)}, u32[]{:S(2)}) copy-start(f32[128]{0:T(128)} %get-tuple-element.30) | copy-start | bytes 1540
  102.7 25.9 %copy-start.23 = (bf16[32,1,128]{2,1,0:T(2,128)(2,1)S(1)}, bf16[32,1,128]{2,1,0:T(2,128)(2,1)}, u32[]{:S(2)}) copy-start(bf16[32,1,128]{2,1,0:T(2,128)(2,1)} %copy.22) | copy-start | bytes 24580
  104.2 53.1 %copy-start.21 = (f32[32,128]{1,0:T(8,128)}, f32[32,128]{1,0:T(8,128)S(1)}, u32[]{:S(2)}) copy-start(f32[32,128]{1,0:T(8,128)S(1)} %convert_reduce_fusion.invp_ref) | copy-start | bytes 49156
  110.1 17.3 %all-to-all-start.1 = ((f32[8,8,128]{2,1,0:T(8,128)}), f32[8,8,128]{2,1,0:T(8,128)S(1)}, u32[]{:S(2)}, u32[]{:S(2)}) async-start(f32[8,8,128]{2,1,0:T(8,128)} %broadcast_in_dim.299), calls=%async_computation.1 | async-start | bytes 65536 | tf_op jit(solution)/shard_map/all_to_all | solution.py:448
  127.5 22.1 %copy-start.24 = (f32[8,128]{1,0:T(8,128)}, f32[8,128]{1,0:T(8,128)S(1)}, u32[]{:S(2)}) copy-start(f32[8,128]{1,0:T(8,128)S(1)} %convert_element_type.155.hard_ref) | copy-start | bytes 12292
  128.4 21.2 %copy-start.42 = (f32[1,128]{1,0:T(1,128)}, f32[1,128]{1,0:T(1,128)S(1)}, u32[]{:S(2)}) copy-start(f32[1,128]{1,0:T(1,128)S(1)} %get-tuple-element.52.cq_ref) | copy-start | bytes 1540
  128.5 21.2 %copy-start.43 = (f32[1,128]{1,0:T(1,128)}, f32[1,128]{1,0:T(1,128)S(1)}, u32[]{:S(2)}) copy-start(f32[1,128]{1,0:T(1,128)S(1)} %get-tuple-element.50.tin_ref) | copy-start | bytes 1540
  130.1 19.5 %all-to-all-start.2 = ((bf16[32,24,128]{2,1,0:T(8,128)(2,1)}), bf16[32,24,128]{2,1,0:T(8,128)(2,1)S(1)}, u32[]{:S(2)}, u32[]{:S(2)}) async-start(bf16[32,24,128]{2,1,0:T(8,128)(2,1)} %concatenate.43), calls=%async_computation.2 | async-start | bytes 393216 | tf_op jit(solution)/shard_map/all_to_all | solution.py:484
  150.3 7.0 %copy-start.1 = (bf16[4,1,512,512]{3,2,1,0:T(8,128)(2,1)S(1)}, bf16[4,1,512,512]{3,2,1,0:T(8,128)(2,1)}, u32[]{:S(2)}) copy-start(bf16[4,1,512,512]{3,2,1,0:T(8,128)(2,1)} %copy-done) | copy-start | bytes 6291460
  157.4 7.9 %copy-start.11 = (bf16[256,512]{1,0:T(8,128)(2,1)S(1)}, bf16[256,512]{1,0:T(8,128)(2,1)}, u32[]{:S(2)}) copy-start(bf16[256,512]{1,0:T(8,128)(2,1)} %get-tuple-element.22) | copy-start | bytes 786436
  159.1 6.1 %collective-permute-start.11 = (bf16[256,2048]{1,0:T(8,128)(2,1)S(1)}, bf16[256,2048]{1,0:T(8,128)(2,1)S(1)}, u32[]{:S(2)}, u32[]{:S(2)}) collective-permute-start(bf16[256,2048]{1,0:T(8,128)(2,1)S(1)} %convolution_convert_fusion), channel_id=1, source_target_pairs={{0,1},{1,0},{2,3},{3,2},{4,5},{5,4},{6,7},{7,6},{8,9},{9,8},{10,11... | collective-permute-start | bytes 3145736 | tf_op jit(solution)/shard_map/ppermute | solution.py:501
  161.9 2.6 %collective-permute-start.15 = (bf16[32,16,128]{2,1,0:T(8,128)(2,1)S(1)}, bf16[32,16,128]{2,1,0:T(8,128)(2,1)S(1)}, u32[]{:S(2)}, u32[]{:S(2)}) collective-permute-start(bf16[32,16,128]{2,1,0:T(8,128)(2,1)S(1)} %slice.66), channel_id=1, source_target_pairs={{0,1},{1,0},{2,3},{3,2},{4,5},{5,4},{6,7},{7,6},{8,9},{9,8},{10,11... | collective-permute-start | bytes 393224 | tf_op jit(solution)/shard_map/ppermute | solution.py:486
  167.5 19.3 %collective-permute-start.14 = (bf16[256,512]{1,0:T(8,128)(2,1)S(1)}, bf16[256,512]{1,0:T(8,128)(2,1)S(1)}, u32[]{:S(2)}, u32[]{:S(2)}) collective-permute-start(bf16[256,512]{1,0:T(8,128)(2,1)S(1)} %get-tuple-element.81), channel_id=1, source_target_pairs={{0,4},{2,6},{4,0},{6,2},{1,5},{3,7},{5,1},{7,3},{8,12},{10,14},{12... | collective-permute-start | bytes 786440 | tf_op jit(solution)/shard_map/ppermute | solution.py:506
  168.7 18.0 %collective-permute-start.13 = (bf16[256,512]{1,0:T(8,128)(2,1)S(1)}, bf16[256,512]{1,0:T(8,128)(2,1)S(1)}, u32[]{:S(2)}, u32[]{:S(2)}) collective-permute-start(bf16[256,512]{1,0:T(8,128)(2,1)S(1)} %get-tuple-element.82), channel_id=1, source_target_pairs={{0,2},{2,4},{4,6},{6,0},{1,3},{3,5},{5,7},{7,1},{8,10},{10,12},{12... | collective-permute-start | bytes 786440 | tf_op jit(solution)/shard_map/ppermute | solution.py:506
  169.1 17.7 %collective-permute-start.12 = (bf16[256,512]{1,0:T(8,128)(2,1)S(1)}, bf16[256,512]{1,0:T(8,128)(2,1)S(1)}, u32[]{:S(2)}, u32[]{:S(2)}) collective-permute-start(bf16[256,512]{1,0:T(8,128)(2,1)S(1)} %get-tuple-element.80), channel_id=1, source_target_pairs={{0,6},{2,0},{4,2},{6,4},{1,7},{3,1},{5,3},{7,5},{8,14},{10,8},{12,... | collective-permute-start | bytes 786440 | tf_op jit(solution)/shard_map/ppermute | solution.py:506
  185.0 3.8 %collective-permute-start.16 = (bf16[2048,128]{1,0:T(8,128)(2,1)}, bf16[2048,128]{1,0:T(8,128)(2,1)S(1)}, u32[]{:S(2)}, u32[]{:S(2)}) collective-permute-start(bf16[2048,128]{1,0:T(8,128)(2,1)} %get-tuple-element.24), channel_id=1, source_target_pairs={{0,1},{1,0},{2,3},{3,2},{4,5},{5,4},{6,7},{7,6},{8,9},{9,8},{10,11... | collective-permute-start | bytes 1572872 | tf_op jit(solution)/shard_map/ppermute | solution.py:510
  186.8 3.1 %collective-permute-start.17 = (bf16[128,4096]{1,0:T(8,128)(2,1)}, bf16[128,4096]{1,0:T(8,128)(2,1)S(1)}, u32[]{:S(2)}, u32[]{:S(2)}) collective-permute-start(bf16[128,4096]{1,0:T(8,128)(2,1)} %get-tuple-element.25.near_ref), channel_id=1, source_target_pairs={{0,1},{1,0},{2,3},{3,2},{4,5},{5,4},{6,7},{7,6},{8,9},{9,8},{10,11... | collective-permute-start | bytes 3145736 | tf_op jit(solution)/shard_map/ppermute | solution.py:511
  (27 other events, 76.4 us)
Sparse Core Ops, SparseCore 0:
  33.4 36.4 all-gather.8
  72.2 64.0 all-gather.6
  138.2 30.9 all-gather.10

commit v2 on v1

--- a/solution.py
+++ b/solution.py
@@ -284,19 +284,24 @@
 
 
 def final_kernel(
-    x_ref, left_ref, near_ref, far_ref, gain_ref, q_ref, p0, p1, p2, p3, p4, out_ref
+    at_ref, mine_ref, other_ref, near_ref, far_ref, gain_ref, q_ref, p0, p1, p2, p3, p4, out_ref
 ):
     step = pl.program_id(0)
-    x = x_ref[0]
+    x, core = at_ref[0], at_ref[1]
 
     @pl.when(step == 0)
     def _():
         out_ref[...] = jnp.zeros_like(out_ref)
 
-    starts = [
-        pl.multiple_of((i * NX + (x + NX - s) % NX) * ROWS, ROWS) for i in range(DEEP) for s in PLACES_X
-    ]
-    left = jnp.concatenate([left_ref[pl.ds(start, ROWS), :] for start in starts], axis=0)
+    per_half = HALF // NX // DEEP
+    is_mine = step // per_half == core
+    left = []
+    for i in range(DEEP):
+        for s in PLACES_X:
+            block = (step % per_half) * DEEP * NX + i * NX + (x + NX - s) % NX
+            at = pl.ds(pl.multiple_of(block * ROWS, ROWS), ROWS)
+            left.append(jnp.where(is_mine, mine_ref[at, :], other_ref[at, :]))
+    left = jnp.concatenate(left, axis=0)
     right = (near_ref[...].astype(F32) + far_ref[...].astype(F32)).astype(BF16)
     out_ref[...] += gain_ref[...] * (
         lax.dot_general(
@@ -307,7 +312,7 @@
     )
 
 
-def final_product(at, left, near, far, gain, q, p):
+def final_product(at, mine, other, near, far, gain, q, p):
     size = DEEP * NX * ROWS
     lanes = lambda n: pl.BlockSpec((n, size), lambda t: (0, t))
     tall = lambda n: pl.BlockSpec((size, n), lambda t: (t, 0))
@@ -315,7 +320,10 @@
         final_kernel,
         grid=(NZ // DEEP,),
         in_specs=[
-            pl.BlockSpec(memory_space=pltpu.SMEM), tall(ROWS), lanes(ROWS), lanes(ROWS),
+            pl.BlockSpec(memory_space=pltpu.SMEM),
+            pl.BlockSpec((HALF * ROWS, ROWS), lambda t: (0, 0)),
+            pl.BlockSpec((HALF * ROWS, ROWS), lambda t: (0, 0)),
+            lanes(ROWS), lanes(ROWS),
             pl.BlockSpec((1, FEATURES), lambda t: (0, 0)), tall(FEATURES),
         ]
         + piece_specs(),
@@ -326,7 +334,7 @@
             flops=2 * 10**9, bytes_accessed=12 * 2**20, transcendentals=0
         ),
         name="final_product",
-    )(at, left, near, far, gain, q, *p)
+    )(at, mine, other, near, far, gain, q, *p)
 
 
 STEPS_Y = (0, 1, 3, 2)
@@ -424,8 +432,9 @@
 
     row_iota = jnp.arange(ROWS, dtype=jnp.int32)
     named = rows_own[:, None, :] == row_iota[None, :, None]
-    *close, share = lax.optimization_barrier(p_pieces[:3] + (share,))
-    p_pieces = tuple(close) + p_pieces[3:]
+    close = lax.optimization_barrier(p_pieces[:3])
+    *distant, share = lax.optimization_barrier(p_pieces[3:] + (share,))
+    p_pieces = tuple(close) + tuple(distant)
     invp_all = jnp.sum(share[:, 50:53].astype(F32), axis=1)
     invp_named = jnp.sum(jnp.where(named, invp_all[:, :, None], 0.0), axis=1)
     raw_hard = jnp.zeros((NEG, ROWS), F32)
@@ -499,21 +508,20 @@
         rounded, w, (((1,), (1,)), ((), ())), preferred_element_type=F32
     )
     came = lax.ppermute(back(proj_other).astype(BF16), "core", shifted(NC, 1))
-    kept = back(proj_mine) + came.astype(F32)
-    grad_attn = kept[:, :FEATURES]
+    kept = lax.optimization_barrier(back(proj_mine)) + came.astype(F32)
+    received = []
     for i, s in list(enumerate(STEPS_Y))[1:]:
         block = kept[:, i * FEATURES : (i + 1) * FEATURES].astype(BF16)
-        grad_attn = grad_attn + lax.ppermute(block, "y", shifted(NY, -s)).astype(F32)
+        received.append(lax.ppermute(block, "y", shifted(NY, -s)))
 
     late_used, _ = lax.optimization_barrier((late_all, kept))
     left, right = coefficients(core, shares, late_used, invp_all)
+    left, right, *received = lax.optimization_barrier((left, right, *received))
+    grad_attn = kept[:, :FEATURES] + sum(v.astype(F32) for v in received)
     left_other = lax.ppermute(left, "core", shifted(NC, 1))
     right_other = lax.ppermute(right, "core", shifted(NC, 1))
-    left = jnp.concatenate(
-        [jnp.where(core == 0, left, left_other), jnp.where(core == 0, left_other, left)], axis=0
-    )
     grad_weight = final_product(
-        x.reshape(1), left, right, right_other, line(gain), q_all, p_pieces
+        jnp.stack([x, core]), left, left_other, right, right_other, line(gain), q_all, p_pieces
     )
     return (
         query_loss,

time: 206 us -> 204 us (level)
    unnamed x112 -> x116, local copies, waits for them, and re-layouts: 4.36 us -> 4.63 us
  transfers between devices with their start and end apart: 24 -> 24, of which waited for: 11 -> 13; matrix products, arithmetic and copies ran while one was open for 17% -> 16% of each run, Pallas kernels for 10% -> 10%
where the time goes in v2:
time: 204 us; the launch traced here: 203 us
  starting transfers between devices  54.6 us (27%)
  waiting for transfers between devices  49.8 us (24%)
  Pallas kernels  27.2 us (13%)
  other arithmetic  17.6 us (9%)
  local copies, waits for them, and re-layouts  15.5 us (8%)
  between operations  15 us (7%)
  blocking collectives  14.1 us (7%)
  matrix products  9.25 us (5%)
    all_gather x1, blocking collectives, body(): total = jnp.sum(lax.all_gather(part, MP, axis=0), axis=0)  14.1 us
    pallas_call x1, Pallas kernels, coefficients(): pl.pallas_call(coef_kernel, grid=(ALL_ROWS // TILE,), in_specs=[pl.BlockS...  13.7 us
    all_to_all x1, starting transfers between devices, body(): raw = jnp.sum(lax.all_to_all(copies, MP, 0, 0, tiled=True), axis=0)  12.7 us
    all_to_all x1, waiting for transfers between devices, body(): share = lax.all_to_all(share, DP, 0, 0, tiled=True)  12.1 us
    ppermute x3, waiting for transfers between devices, body(): lax.ppermute(block, 'y', shifted(NY, s))  10.7 us
    all_to_all x1, starting transfers between devices, body(): came = lax.all_to_all(came, DP, 0, 0, tiled=True)  9.35 us
    all_to_all x1, waiting for transfers between devices, body(): came = lax.all_to_all(came, DP, 0, 0, tiled=True)  9.28 us
    all_to_all x1, starting transfers between devices, body(): share = lax.all_to_all(share, DP, 0, 0, tiled=True)  8.13 us
  transfers between devices with their start and end apart: 24, of which 13 were waited for; matrix products, arithmetic and copies ran while one was open for 16% of the time, Pallas kernels for 10%

profile of v2, /device:TPU:1, one launch (start us, length us, event | category | flops | bytes accessed | tf_op | source)
XLA Modules:
  0.0 203.0 jit_solution(8165024581612773337)
XLA Ops:
  7.2 3.8 %collective-permute-start.2 = (bf16[256,512]{1,0:T(8,128)(2,1)}, bf16[256,512]{1,0:T(8,128)(2,1)S(1)}, u32[]{:S(2)}, u32[]{:S(2)}) collective-permute-start(bf16[256,512]{1,0:T(8,128)(2,1)} %bitcast.178), channel_id=1, source_target_pairs={{0,4},{2,6},{4,0},{6,2},{1,5},{3,7},{5,1},{7,3},{8,12},{10,14},{12... | collective-permute-start | bytes 786440 | tf_op jit(solution)/shard_map/ppermute | solution.py:360
  11.0 0.8 collective-permute-start.1
  12.5 3.9 %collective-permute-done.2 = bf16[256,512]{1,0:T(8,128)(2,1)S(1)} collective-permute-done((bf16[256,512]{1,0:T(8,128)(2,1)}, bf16[256,512]{1,0:T(8,128)(2,1)S(1)}, u32[]{:S(2)}, u32[]{:S(2)}) %collective-permute-start.2) | collective-permute-done | bytes 262176 | tf_op jit(solution)/shard_map/ppermute | solution.py:360
  16.4 6.7 %collective-permute-done.1 = bf16[256,512]{1,0:T(8,128)(2,1)S(1)} collective-permute-done((bf16[256,512]{1,0:T(8,128)(2,1)}, bf16[256,512]{1,0:T(8,128)(2,1)S(1)}, u32[]{:S(2)}, u32[]{:S(2)}) %collective-permute-start.1) | collective-permute-done | bytes 262176 | tf_op jit(solution)/shard_map/ppermute | solution.py:360
  23.2 1.2 pad_maximum_fusion.2
  24.4 1.5 collective-permute-start.3
  25.9 2.4 %constant_dynamic-slice_fusion.18 = (bf16[1,1,512,512]{3,2,1,0:T(8,128)(2,1)S(1)}, bf16[1,1,512,512]{3,2,1,0:T(8,128)(2,1)S(1)}, bf16[1,1,512,512]{3,2,1,0:T(8,1...) fusion(bf16[4,2,512,512]{3,2,1,0:T(8,128)(2,1)} %bitcast.165, ...), kind=kLoop, calls=%fused_computation.126 | loop fusion | bytes 8388632 | tf_op jit(solution)/shard_map/dynamic_slice | solution.py:352
  29.0 2.7 %fusion.56 = f32[256,512]{1,0:T(8,128)S(1)} fusion(bf16[256,2048]{1,0:T(8,128)(2,1)} %collective-permute-done.3, bf16[2048,512]{1,0:T(8,128)(2,1)S(1)} %bitcast.158), kind=kOutput, calls=%fused_computation.213 | convolution fusion | flops 536870912 | bytes 3670016 | tf_op jit(solution)/shard_map/dot_general | solution.py:364
  33.4 1.3 collective-permute-start.4
  34.7 1.5 collective-permute-start.5
  36.2 1.5 collective-permute-start.6
  37.7 1.8 collective-permute-done.4
  39.6 3.7 %collective-permute-done.6 = bf16[128,512]{1,0:T(8,128)(2,1)S(1)} collective-permute-done((bf16[128,512]{1,0:T(8,128)(2,1)S(1)}, bf16[128,512]{1,0:T(8,128)(2,1)S(1)}, u32[]{:S(2)}, u32[]{:S(2)}) %collective-permute-start.6) | collective-permute-done | bytes 131104 | tf_op jit(solution)/shard_map/ppermute | solution.py:37
  43.3 0.8 copy-done.8
  49.3 1.0 broadcast_select_fusion.4
  51.9 0.8 multiply_reduce_fusion.1
  52.8 14.1 %all-gather = f32[1088,128]{1,0:T(8,128)S(1)} all-gather(f32[136,128]{1,0:T(8,128)S(1)} %maximum_maximum_fusion), channel_id=2, replica_groups=mesh['z'=8,'x'=4,'y'=4,'core'=2] {'y','core'}, dimensions={0}, use_global_device_ids=true | all-gather | bytes 626688 | tf_op jit(solution)/shard_map/all_gather | solution.py:403
  69.0 0.9 all-gather.9.cloned.1.call-done
  69.9 1.2 collective-permute-start.7
  71.1 1.5 collective-permute-start.8
  73.9 0.8 pad_maximum_fusion.3
  74.7 8.1 %all-to-all-start = ((bf16[32,56,128]{2,1,0:T(8,128)(2,1)}), bf16[32,56,128]{2,1,0:T(8,128)(2,1)}, u32[]{:S(2)}, u32[]{:S(2)}) async-start(bf16[32,56,128]{2,1,0:T(8,128)(2,1)} %pad_maximum_fusion.3), calls=%async_computation | async-start | bytes 917504 | tf_op jit(solution)/shard_map/all_to_all | solution.py:430
  83.6 12.1 %all-to-all-done = bf16[32,56,128]{2,1,0:T(8,128)(2,1)} async-done(((bf16[32,56,128]{2,1,0:T(8,128)(2,1)}), bf16[32,56,128]{2,1,0:T(8,128)(2,1)}, u32[]{:S(2)}, u32[]{:S(2)}) %all-to-all-start) | async-done | bytes 458784 | tf_op jit(solution)/shard_map/all_to_all | solution.py:430
  95.7 2.2 %collective-permute-start.9 = (bf16[4,128,512]{2,1,0:T(8,128)(2,1)S(1)}, bf16[4,128,512]{2,1,0:T(8,128)(2,1)S(1)}, u32[]{:S(2)}, u32[]{:S(2)}) collective-permute-start(bf16[4,128,512]{2,1,0:T(8,128)(2,1)S(1)} %slice.60), channel_id=1, source_target_pairs={{0,8},{8,16},{16,24},{24,0},{1,9},{9,17},{17,25},{25,1},{2,10},{10... | collective-permute-start | bytes 1572872 | tf_op jit(solution)/shard_map/ppermute | solution.py:47
  97.9 1.1 slice.61
  99.0 1.4 collective-permute-start.10
  100.8 1.7 fusion.4
  103.2 4.0 %collective-permute-done.9.p3 = bf16[4,128,512]{2,1,0:T(8,128)(2,1)S(1)} collective-permute-done((bf16[4,128,512]{2,1,0:T(8,128)(2,1)S(1)}, bf16[4,128,512]{2,1,0:T(8,128)(2,1)S(1)}, u32[]{:S(2)}, u32[]{:S(2)}) %collective-permute-start.9) | collective-permute-done | bytes 524320 | tf_op jit(solution)/shard_map/ppermute | solution.py:47
  109.8 12.7 %all-to-all-start.1 = ((f32[8,8,128]{2,1,0:T(8,128)}), f32[8,8,128]{2,1,0:T(8,128)S(1)}, u32[]{:S(2)}, u32[]{:S(2)}) async-start(f32[8,8,128]{2,1,0:T(8,128)} %broadcast_in_dim.299), calls=%async_computation.1 | async-start | bytes 65536 | tf_op jit(solution)/shard_map/all_to_all | solution.py:457
  122.5 0.9 convert_reduce_fusion.invp_ref
  124.2 3.1 %all-to-all-done.1 = f32[8,8,128]{2,1,0:T(8,128)S(1)} async-done(((f32[8,8,128]{2,1,0:T(8,128)}), f32[8,8,128]{2,1,0:T(8,128)S(1)}, u32[]{:S(2)}, u32[]{:S(2)}) %all-to-all-start.1) | async-done | bytes 32800 | tf_op jit(solution)/shard_map/all_to_all | solution.py:457
  129.0 1.4 concatenate.40
  130.4 9.3 %all-to-all-start.2 = ((bf16[32,24,128]{2,1,0:T(8,128)(2,1)}), bf16[32,24,128]{2,1,0:T(8,128)(2,1)S(1)}, u32[]{:S(2)}, u32[]{:S(2)}) async-start(bf16[32,24,128]{2,1,0:T(8,128)(2,1)} %concatenate.40), calls=%async_computation.2 | async-start | bytes 393216 | tf_op jit(solution)/shard_map/all_to_all | solution.py:493
  140.4 9.3 %all-to-all-done.2.came_ref = bf16[32,24,128]{2,1,0:T(8,128)(2,1)S(1)} async-done(((bf16[32,24,128]{2,1,0:T(8,128)(2,1)}), bf16[32,24,128]{2,1,0:T(8,128)(2,1)S(1)}, u32[]{:S(2)}, u32[]{:S(2)}) %all-to-all-start.2) | async-done | bytes 196640 | tf_op jit(solution)/shard_map/all_to_all | solution.py:493
  150.4 7.0 %own_gradients.1 = (f32[256,512]{1,0:T(8,128)}, bf16[256,512]{1,0:T(8,128)(2,1)}) custom-call(s32[2]{0:T(128)} %pad_add_fusion.d_ref, s32[8,128]{1,0:T(8,128)} %bitcast.170, s32[8,128]{1,0:T(8,128)} %bitcast.192, f32[8,128]{1,0:T(8,128)} %copy-done.24, f32[128,128]{1,0:T(8,128)} %get-tuple-element.113.inner_ref, bf16[32,24,128]{2,1,0:T(8,128)(2,1)} %copy-done.4, ...), custom_call_target="tpu_custom_call" | custom-call | flops 2000000000 | bytes 10485760 | tf_op jit(solution)/shard_map/own_gradients/pallas_call | solution.py:259
  157.4 1.8 convolution_convert_fusion
  159.2 2.8 %collective-permute-start.11 = (bf16[256,2048]{1,0:T(8,128)(2,1)S(1)}, bf16[256,2048]{1,0:T(8,128)(2,1)S(1)}, u32[]{:S(2)}, u32[]{:S(2)}) collective-permute-start(bf16[256,2048]{1,0:T(8,128)(2,1)S(1)} %convolution_convert_fusion), channel_id=1, source_target_pairs={{0,1},{1,0},{2,3},{3,2},{4,5},{5,4},{6,7},{7,6},{8,9},{9,8},{10,11... | collective-permute-start | bytes 3145736 | tf_op jit(solution)/shard_map/ppermute | solution.py:510
  162.1 2.5 %collective-permute-done.12 = bf16[32,16,128]{2,1,0:T(8,128)(2,1)S(1)} collective-permute-done((bf16[32,16,128]{2,1,0:T(8,128)(2,1)S(1)}, bf16[32,16,128]{2,1,0:T(8,128)(2,1)S(1)}, u32[]{:S(2)}, u32[]{:S(2)}) %collective-permute-start.12) | collective-permute-done | bytes 131104 | tf_op jit(solution)/shard_map/ppermute | solution.py:495
  166.5 0.8 fusion.53
  167.3 1.0 collective-permute-start.13
  168.8 1.2 collective-permute-start.15
  170.0 13.7 %coefficients.1 = (bf16[2048,128]{1,0:T(8,128)(2,1)}, bf16[128,4096]{1,0:T(8,128)(2,1)}) custom-call(s32[1]{0:T(128)} %bitcast.38.core_ref, bf16[8,32,56,128]{3,2,1,0:T(8,128)(2,1)} %bitcast.202, bf16[32,32,128]{2,1,0:T(8,128)(2,1)} %pad_maximum_fusion.4.late_ref.whole_ref, bf16[8,32,56,128]{3,2,1,0:T(8,128)(2,1)} %bitcast.203, ...), custom_call_target="tpu_custom_call" | custom-call | flops 10000000000 | bytes 8388608 | tf_op jit(solution)/shard_map/coefficients/pallas_call | solution.py:178
  183.7 1.3 collective-permute-start.17
  186.2 0.9 slice_add_fusion
  187.1 1.1 collective-permute-done.16.other_ref
  188.2 0.8 copy-done.12
  189.0 1.0 copy-done.10
  190.0 6.5 %final_product.1 = f32[128,512]{1,0:T(8,128)} custom-call(s32[2]{0:T(128)} %pad_add_fusion.1.at_ref, bf16[2048,128]{1,0:T(8,128)(2,1)} %get-tuple-element.38.mine_ref, bf16[2048,128]{1,0:T(8,128)(2,1)} %copy-done.12, bf16[128,4096]{1,0:T(8,128)(2,1)} %get-tuple-element.39.near_ref, bf16[128,4096]{1,0:T(8,128)(2,1)} %copy-done.10, f32[1,512]{1,0:T(1,128)} %bitcast.198, ...), custom_call_target="tpu_custom_call" | custom-call | flops 2000000000 | bytes 12582912 | tf_op jit(solution)/shard_map/final_product/pallas_call | solution.py:319
  (230 shorter events, 24.6 us)
Async XLA Ops:
  7.2 62.7 %all-gather.9.cloned.1.call-start = ((), (), s32[]{:S(2)}) async-start(), calls=%async_computation.4 | async-start | bytes 1179648 | tf_op jit(solution)/shard_map/all_gather | solution.py:369
  7.2 9.2 %collective-permute-start.2 = (bf16[256,512]{1,0:T(8,128)(2,1)}, bf16[256,512]{1,0:T(8,128)(2,1)S(1)}, u32[]{:S(2)}, u32[]{:S(2)}) collective-permute-start(bf16[256,512]{1,0:T(8,128)(2,1)} %bitcast.178), channel_id=1, source_target_pairs={{0,4},{2,6},{4,0},{6,2},{1,5},{3,7},{5,1},{7,3},{8,12},{10,14},{12... | collective-permute-start | bytes 786440 | tf_op jit(solution)/shard_map/ppermute | solution.py:360
  11.0 12.1 %collective-permute-start.1 = (bf16[256,512]{1,0:T(8,128)(2,1)}, bf16[256,512]{1,0:T(8,128)(2,1)S(1)}, u32[]{:S(2)}, u32[]{:S(2)}) collective-permute-start(bf16[256,512]{1,0:T(8,128)(2,1)} %bitcast.179), channel_id=1, source_target_pairs={{0,6},{2,0},{4,2},{6,4},{1,7},{3,1},{5,3},{7,5},{8,14},{10,8},{12,... | collective-permute-start | bytes 786440 | tf_op jit(solution)/shard_map/ppermute | solution.py:360
  11.8 11.4 %collective-permute-start = (bf16[256,512]{1,0:T(8,128)(2,1)}, bf16[256,512]{1,0:T(8,128)(2,1)S(1)}, u32[]{:S(2)}, u32[]{:S(2)}) collective-permute-start(bf16[256,512]{1,0:T(8,128)(2,1)} %bitcast.180), channel_id=1, source_target_pairs={{0,2},{2,4},{4,6},{6,0},{1,3},{3,5},{5,7},{7,1},{8,10},{10,12},{12... | collective-permute-start | bytes 786440 | tf_op jit(solution)/shard_map/ppermute | solution.py:360
  24.4 4.6 %collective-permute-start.3 = (bf16[256,2048]{1,0:T(8,128)(2,1)S(1)}, bf16[256,2048]{1,0:T(8,128)(2,1)}, u32[]{:S(2)}, u32[]{:S(2)}) collective-permute-start(bf16[256,2048]{1,0:T(8,128)(2,1)S(1)} %pad_maximum_fusion.2), channel_id=1, source_target_pairs={{0,1},{1,0},{2,3},{3,2},{4,5},{5,4},{6,7},{7,6},{8,9},{9,8},{10,11... | collective-permute-start | bytes 3145736 | tf_op jit(solution)/shard_map/ppermute | solution.py:362
  32.5 11.7 %copy-start.15 = (s32[128,8]{0,1:T(8,128)S(1)}, s32[128,8]{0,1:T(8,128)}, u32[]{:S(2)}) copy-start(s32[128,8]{0,1:T(8,128)} %param.10) | copy-start | bytes 12292
  32.5 11.7 %copy-start.25 = (s32[128,8]{0,1:T(8,128)S(1)}, s32[128,8]{0,1:T(8,128)}, u32[]{:S(2)}) copy-start(s32[128,8]{0,1:T(8,128)} %param.11) | copy-start | bytes 12292
  33.3 116.4 %all-gather.7.cloned.1.call-start = ((), (), s32[]{:S(2)}) async-start(), calls=%async_computation.3 | async-start | bytes 4718592 | tf_op jit(solution)/shard_map/all_gather | solution.py:373
  33.4 18.3 %copy-start.13 = (bf16[128,512]{1,0:T(8,128)(2,1)}, bf16[128,512]{1,0:T(8,128)(2,1)S(1)}, u32[]{:S(2)}) copy-start(bf16[128,512]{1,0:T(8,128)(2,1)S(1)} %get-tuple-element.81) | copy-start | bytes 393220
  33.4 6.1 %collective-permute-start.4 = (bf16[128,512]{1,0:T(8,128)(2,1)S(1)}, bf16[128,512]{1,0:T(8,128)(2,1)S(1)}, u32[]{:S(2)}, u32[]{:S(2)}) collective-permute-start(bf16[128,512]{1,0:T(8,128)(2,1)S(1)} %get-tuple-element.81), channel_id=1, source_target_pairs={{0,8},{8,16},{16,24},{24,0},{1,9},{9,17},{17,25},{25,1},{2,10},{10... | collective-permute-start | bytes 393224 | tf_op jit(solution)/shard_map/ppermute | solution.py:37
  34.7 4.8 %collective-permute-start.5 = (bf16[128,512]{1,0:T(8,128)(2,1)S(1)}, bf16[128,512]{1,0:T(8,128)(2,1)S(1)}, u32[]{:S(2)}, u32[]{:S(2)}) collective-permute-start(bf16[128,512]{1,0:T(8,128)(2,1)S(1)} %get-tuple-element.81), channel_id=1, source_target_pairs={{0,24},{8,0},{16,8},{24,16},{1,25},{9,1},{17,9},{25,17},{2,26},{10... | collective-permute-start | bytes 393224 | tf_op jit(solution)/shard_map/ppermute | solution.py:37
  36.2 7.1 %collective-permute-start.6 = (bf16[128,512]{1,0:T(8,128)(2,1)S(1)}, bf16[128,512]{1,0:T(8,128)(2,1)S(1)}, u32[]{:S(2)}, u32[]{:S(2)}) collective-permute-start(bf16[128,512]{1,0:T(8,128)(2,1)S(1)} %get-tuple-element.81), channel_id=1, source_target_pairs={{0,16},{8,24},{16,0},{24,8},{1,17},{9,25},{17,1},{25,9},{2,18},{10... | collective-permute-start | bytes 393224 | tf_op jit(solution)/shard_map/ppermute | solution.py:37
  52.7 30.8 %copy-start.27 = (s32[8,128]{1,0:T(8,128)S(1)}, s32[8,128]{1,0:T(8,128)}, u32[]{:S(2)}) copy-start(s32[8,128]{1,0:T(8,128)} %get-tuple-element.46) | copy-start | bytes 12292
  52.7 30.8 %copy-start.28 = (s32[8,128]{1,0:T(8,128)S(1)}, s32[8,128]{1,0:T(8,128)}, u32[]{:S(2)}) copy-start(s32[8,128]{1,0:T(8,128)} %get-tuple-element.47) | copy-start | bytes 12292
  67.6 31.4 %copy-start.29 = (f32[128]{0:T(128)}, f32[128]{0:T(128)S(1)}, u32[]{:S(2)}) copy-start(f32[128]{0:T(128)S(1)} %get-tuple-element.112) | copy-start | bytes 1540
  67.6 61.2 %copy-start.26 = (f32[1,128]{1,0:T(1,128)}, f32[1,128]{1,0:T(1,128)S(1)}, u32[]{:S(2)}) copy-start(f32[1,128]{1,0:T(1,128)S(1)} %get-tuple-element.77.invp_ref) | copy-start | bytes 1540
  67.7 31.3 %copy-start.31 = (f32[128]{0:T(128)}, f32[128]{0:T(128)S(1)}, u32[]{:S(2)}) copy-start(f32[128]{0:T(128)S(1)} %fusion.48) | copy-start | bytes 1540
  69.9 25.8 %collective-permute-start.7 = (bf16[8,128,512]{2,1,0:T(8,128)(2,1)}, bf16[8,128,512]{2,1,0:T(8,128)(2,1)S(1)}, u32[]{:S(2)}, u32[]{:S(2)}) collective-permute-start(bf16[8,128,512]{2,1,0:T(8,128)(2,1)} %bitcast.160), channel_id=1, source_target_pairs={{0,8},{8,16},{16,24},{24,0},{1,9},{9,17},{17,25},{25,1},{2,10},{10... | collective-permute-start | bytes 3145736 | tf_op jit(solution)/shard_map/ppermute | solution.py:45
  71.1 26.8 %collective-permute-start.8 = (bf16[8,128,512]{2,1,0:T(8,128)(2,1)}, bf16[8,128,512]{2,1,0:T(8,128)(2,1)}, u32[]{:S(2)}, u32[]{:S(2)}) collective-permute-start(bf16[8,128,512]{2,1,0:T(8,128)(2,1)} %bitcast.161), channel_id=1, source_target_pairs={{0,24},{8,0},{16,8},{24,16},{1,25},{9,1},{17,9},{25,17},{2,26},{10... | collective-permute-start | bytes 3145736 | tf_op jit(solution)/shard_map/ppermute | solution.py:46
  74.7 25.7 %copy-start.14 = (bf16[128,512]{1,0:T(8,128)(2,1)S(1)}, bf16[128,512]{1,0:T(8,128)(2,1)}, u32[]{:S(2)}) copy-start(bf16[128,512]{1,0:T(8,128)(2,1)} %copy-done.13) | copy-start | bytes 393220
  74.7 20.9 %all-to-all-start = ((bf16[32,56,128]{2,1,0:T(8,128)(2,1)}), bf16[32,56,128]{2,1,0:T(8,128)(2,1)}, u32[]{:S(2)}, u32[]{:S(2)}) async-start(bf16[32,56,128]{2,1,0:T(8,128)(2,1)} %pad_maximum_fusion.3), calls=%async_computation | async-start | bytes 917504 | tf_op jit(solution)/shard_map/all_to_all | solution.py:430
  82.8 87.1 %all-gather.11.cloned.1.call-start = ((), (), s32[]{:S(2)}) async-start(), calls=%async_computation.5 | async-start | bytes 4128768 | tf_op jit(solution)/shard_map/all_gather | solution.py:431
  95.7 6.8 %copy-start.2 = (bf16[8,128,512]{2,1,0:T(8,128)(2,1)}, bf16[8,128,512]{2,1,0:T(8,128)(2,1)S(1)}, u32[]{:S(2)}) copy-start(bf16[8,128,512]{2,1,0:T(8,128)(2,1)S(1)} %collective-permute-done.7.p1) | copy-start | bytes 3145732
  95.7 11.4 %collective-permute-start.9 = (bf16[4,128,512]{2,1,0:T(8,128)(2,1)S(1)}, bf16[4,128,512]{2,1,0:T(8,128)(2,1)S(1)}, u32[]{:S(2)}, u32[]{:S(2)}) collective-permute-start(bf16[4,128,512]{2,1,0:T(8,128)(2,1)S(1)} %slice.60), channel_id=1, source_target_pairs={{0,8},{8,16},{16,24},{24,0},{1,9},{9,17},{17,25},{25,1},{2,10},{10... | collective-permute-start | bytes 1572872 | tf_op jit(solution)/shard_map/ppermute | solution.py:47
  99.0 8.7 %collective-permute-start.10 = (bf16[4,128,512]{2,1,0:T(8,128)(2,1)S(1)}, bf16[4,128,512]{2,1,0:T(8,128)(2,1)S(1)}, u32[]{:S(2)}, u32[]{:S(2)}) collective-permute-start(bf16[4,128,512]{2,1,0:T(8,128)(2,1)S(1)} %slice.61), channel_id=1, source_target_pairs={{0,24},{8,0},{16,8},{24,16},{1,25},{9,1},{17,9},{25,17},{2,26},{10... | collective-permute-start | bytes 1572872 | tf_op jit(solution)/shard_map/ppermute | solution.py:48
  100.8 7.1 %copy-start.45 = (s32[4,128]{1,0:T(4,128)S(1)}, s32[4,128]{1,0:T(4,128)}, u32[]{:S(2)}) copy-start(s32[4,128]{1,0:T(4,128)} %broadcast_add_fusion.6) | copy-start | bytes 6148
  102.5 20.9 %copy-start.22 = (s32[32,128]{1,0:T(8,128)S(1)}, s32[32,128]{1,0:T(8,128)}, u32[]{:S(2)}) copy-start(s32[32,128]{1,0:T(8,128)} %get-tuple-element.117) | copy-start | bytes 49156
  102.6 24.8 %copy-start.30 = (f32[128]{0:T(128)S(1)}, f32[128]{0:T(128)}, u32[]{:S(2)}) copy-start(f32[128]{0:T(128)} %copy-done.29) | copy-start | bytes 1540
  102.6 24.8 %copy-start.32 = (f32[128]{0:T(128)S(1)}, f32[128]{0:T(128)}, u32[]{:S(2)}) copy-start(f32[128]{0:T(128)} %copy-done.31) | copy-start | bytes 1540
  102.6 24.8 %copy-start.34 = (f32[128]{0:T(128)S(1)}, f32[128]{0:T(128)}, u32[]{:S(2)}) copy-start(f32[128]{0:T(128)} %get-tuple-element.45) | copy-start | bytes 1540
  102.6 24.8 %copy-start.44 = (f32[128]{0:T(128)S(1)}, f32[128]{0:T(128)}, u32[]{:S(2)}) copy-start(f32[128]{0:T(128)} %get-tuple-element.44) | copy-start | bytes 1540
  102.6 26.4 %copy-start.23 = (bf16[32,1,128]{2,1,0:T(2,128)(2,1)S(1)}, bf16[32,1,128]{2,1,0:T(2,128)(2,1)}, u32[]{:S(2)}) copy-start(bf16[32,1,128]{2,1,0:T(2,128)(2,1)} %copy.22) | copy-start | bytes 24580
  109.8 17.5 %all-to-all-start.1 = ((f32[8,8,128]{2,1,0:T(8,128)}), f32[8,8,128]{2,1,0:T(8,128)S(1)}, u32[]{:S(2)}, u32[]{:S(2)}) async-start(f32[8,8,128]{2,1,0:T(8,128)} %broadcast_in_dim.299), calls=%async_computation.1 | async-start | bytes 65536 | tf_op jit(solution)/shard_map/all_to_all | solution.py:457
  123.4 33.9 %copy-start.21 = (f32[32,128]{1,0:T(8,128)}, f32[32,128]{1,0:T(8,128)S(1)}, u32[]{:S(2)}) copy-start(f32[32,128]{1,0:T(8,128)S(1)} %convert_reduce_fusion.invp_ref) | copy-start | bytes 49156
  127.5 22.2 %copy-start.24 = (f32[8,128]{1,0:T(8,128)}, f32[8,128]{1,0:T(8,128)S(1)}, u32[]{:S(2)}) copy-start(f32[8,128]{1,0:T(8,128)S(1)} %convert_element_type.155.hard_ref) | copy-start | bytes 12292
  128.7 21.0 %copy-start.42 = (f32[1,128]{1,0:T(1,128)}, f32[1,128]{1,0:T(1,128)S(1)}, u32[]{:S(2)}) copy-start(f32[1,128]{1,0:T(1,128)S(1)} %get-tuple-element.68.cq_ref) | copy-start | bytes 1540
  128.8 20.9 %copy-start.43 = (f32[1,128]{1,0:T(1,128)}, f32[1,128]{1,0:T(1,128)S(1)}, u32[]{:S(2)}) copy-start(f32[1,128]{1,0:T(1,128)S(1)} %get-tuple-element.66.tin_ref) | copy-start | bytes 1540
  130.4 19.3 %all-to-all-start.2 = ((bf16[32,24,128]{2,1,0:T(8,128)(2,1)}), bf16[32,24,128]{2,1,0:T(8,128)(2,1)S(1)}, u32[]{:S(2)}, u32[]{:S(2)}) async-start(bf16[32,24,128]{2,1,0:T(8,128)(2,1)} %concatenate.40), calls=%async_computation.2 | async-start | bytes 393216 | tf_op jit(solution)/shard_map/all_to_all | solution.py:493
  150.4 7.0 %copy-start.1 = (bf16[4,1,512,512]{3,2,1,0:T(8,128)(2,1)S(1)}, bf16[4,1,512,512]{3,2,1,0:T(8,128)(2,1)}, u32[]{:S(2)}) copy-start(bf16[4,1,512,512]{3,2,1,0:T(8,128)(2,1)} %copy-done) | copy-start | bytes 6291460
  157.4 8.0 %copy-start.11 = (bf16[256,512]{1,0:T(8,128)(2,1)S(1)}, bf16[256,512]{1,0:T(8,128)(2,1)}, u32[]{:S(2)}) copy-start(bf16[256,512]{1,0:T(8,128)(2,1)} %get-tuple-element.31) | copy-start | bytes 786436
  159.2 6.9 %collective-permute-start.11 = (bf16[256,2048]{1,0:T(8,128)(2,1)S(1)}, bf16[256,2048]{1,0:T(8,128)(2,1)S(1)}, u32[]{:S(2)}, u32[]{:S(2)}) collective-permute-start(bf16[256,2048]{1,0:T(8,128)(2,1)S(1)} %convolution_convert_fusion), channel_id=1, source_target_pairs={{0,1},{1,0},{2,3},{3,2},{4,5},{5,4},{6,7},{7,6},{8,9},{9,8},{10,11... | collective-permute-start | bytes 3145736 | tf_op jit(solution)/shard_map/ppermute | solution.py:510
  162.0 2.6 %collective-permute-start.12 = (bf16[32,16,128]{2,1,0:T(8,128)(2,1)S(1)}, bf16[32,16,128]{2,1,0:T(8,128)(2,1)S(1)}, u32[]{:S(2)}, u32[]{:S(2)}) collective-permute-start(bf16[32,16,128]{2,1,0:T(8,128)(2,1)S(1)} %slice.63), channel_id=1, source_target_pairs={{0,1},{1,0},{2,3},{3,2},{4,5},{5,4},{6,7},{7,6},{8,9},{9,8},{10,11... | collective-permute-start | bytes 393224 | tf_op jit(solution)/shard_map/ppermute | solution.py:495
  167.3 16.3 %collective-permute-start.13 = (bf16[256,512]{1,0:T(8,128)(2,1)}, bf16[256,512]{1,0:T(8,128)(2,1)S(1)}, u32[]{:S(2)}, u32[]{:S(2)}) collective-permute-start(bf16[256,512]{1,0:T(8,128)(2,1)} %get-tuple-element.96), channel_id=1, source_target_pairs={{0,6},{2,0},{4,2},{6,4},{1,7},{3,1},{5,3},{7,5},{8,14},{10,8},{12,... | collective-permute-start | bytes 786440 | tf_op jit(solution)/shard_map/ppermute | solution.py:515
  168.3 15.4 %collective-permute-start.14 = (bf16[256,512]{1,0:T(8,128)(2,1)S(1)}, bf16[256,512]{1,0:T(8,128)(2,1)S(1)}, u32[]{:S(2)}, u32[]{:S(2)}) collective-permute-start(bf16[256,512]{1,0:T(8,128)(2,1)S(1)} %get-tuple-element.95), channel_id=1, source_target_pairs={{0,2},{2,4},{4,6},{6,0},{1,3},{3,5},{5,7},{7,1},{8,10},{10,12},{12... | collective-permute-start | bytes 786440 | tf_op jit(solution)/shard_map/ppermute | solution.py:515
  168.8 14.9 %collective-permute-start.15 = (bf16[256,512]{1,0:T(8,128)(2,1)S(1)}, bf16[256,512]{1,0:T(8,128)(2,1)S(1)}, u32[]{:S(2)}, u32[]{:S(2)}) collective-permute-start(bf16[256,512]{1,0:T(8,128)(2,1)S(1)} %get-tuple-element.94), channel_id=1, source_target_pairs={{0,4},{2,6},{4,0},{6,2},{1,5},{3,7},{5,1},{7,3},{8,12},{10,14},{12... | collective-permute-start | bytes 786440 | tf_op jit(solution)/shard_map/ppermute | solution.py:515
  170.0 15.7 %copy-start.47 = (f32[128]{0:T(128)S(1)}, f32[128]{0:T(128)}, u32[]{:S(2)}) copy-start(f32[128]{0:T(128)} %copy-done.46) | copy-start | bytes 1540
  183.7 4.6 %collective-permute-start.17 = (bf16[128,4096]{1,0:T(8,128)(2,1)}, bf16[128,4096]{1,0:T(8,128)(2,1)S(1)}, u32[]{:S(2)}, u32[]{:S(2)}) collective-permute-start(bf16[128,4096]{1,0:T(8,128)(2,1)} %get-tuple-element.39.near_ref), channel_id=1, source_target_pairs={{0,1},{1,0},{2,3},{3,2},{4,5},{5,4},{6,7},{7,6},{8,9},{9,8},{10,11... | collective-permute-start | bytes 3145736 | tf_op jit(solution)/shard_map/ppermute | solution.py:522
  185.0 3.2 %collective-permute-start.16 = (bf16[2048,128]{1,0:T(8,128)(2,1)}, bf16[2048,128]{1,0:T(8,128)(2,1)S(1)}, u32[]{:S(2)}, u32[]{:S(2)}) collective-permute-start(bf16[2048,128]{1,0:T(8,128)(2,1)} %get-tuple-element.38.mine_ref), channel_id=1, source_target_pairs={{0,1},{1,0},{2,3},{3,2},{4,5},{5,4},{6,7},{7,6},{8,9},{9,8},{10,11... | collective-permute-start | bytes 1572872 | tf_op jit(solution)/shard_map/ppermute | solution.py:521
  (29 other events, 83.5 us)
Sparse Core Ops, SparseCore 0:
  33.4 36.4 all-gather.8
  72.3 64.0 all-gather.6
  138.2 30.9 all-gather.10
